TPU v7x, 256 devices: a whole 4x4x8 slice. The times are simulated.
256 devices in a mesh: lon: 16 (over z, x_hi), lat: 16 (over y, x_lo, core).
Axes of the slice: x: 4 (x_hi: 2, x_lo: 2; x = x_hi * 2 + x_lo), y: 4, z: 8, core: 2. Of those that a mesh axis runs over, the one named last changes fastest.
Arguments:
- temp: float32 [48, 256, 2048], P(None, 'lat', 'lon'), may hold values from -6 to 6
- salt: float32 [48, 256, 2048], P(None, 'lat', 'lon'), may hold values from -6 to 6
- east_speed: float32 [48, 256, 2048], P(None, 'lat', 'lon'), may hold values from -0.15 to 0.15
- north_speed: float32 [48, 256, 2048], P(None, 'lat', 'lon'), may hold values from -0.15 to 0.15
- mixing_h: float32 [48, 256, 2048], P(None, 'lat', 'lon'), may hold values from 0.01 to 0.08
- mixing_v: float32 [48, 256, 2048], P(None, 'lat', 'lon'), may hold values from 0.1 to 10
- wet: int32 [48, 256, 2048], P(None, 'lat', 'lon'), may hold values from 0 to 1, as said below
- bottom: int32 [256, 2048], P('lat', 'lon'), may hold values from 0 to 48, as said below
Outputs:
- temp_out: float32 [48, 256, 2048], P(None, 'lat', 'lon')
- salt_out: float32 [48, 256, 2048], P(None, 'lat', 'lon')
Inputs may be any that keep to these rules, and one draw needn't show every extreme that they name: wet[k, y, x] is 1 exactly where k < bottom[y, x]. `bottom`: 0 marks land columns; every draw has land columns and columns 48 levels deep.
All inputs are finite; a program needn't handle non-finite values.
Results may differ from a plain program's by a relative error of at most 0.00002.
Values sent between devices are 32-bit elements; how exact they have to be, the bound alone decides.
No kernel may reach another device: no remote copies, remote signals or barrier semaphores. Data moves between devices by JAX's collectives and lax.ppermute only.
A program may use at most 128 MiB of HBM per device.

v0:
```python
import functools

import jax
import jax.numpy as jnp
from jax import lax
from jax.experimental import pallas as pl
from jax.experimental.pallas import tpu as pltpu
from jax.sharding import PartitionSpec as P

F32 = jnp.float32
NF = 8


def lat_routes(count_lon, count_lat):
    first, second = [], []
    for i in range(count_lon):
        for j in range(count_lat):
            here = i * count_lat + j
            upward, downward = (first, second) if j % 2 else (second, first)
            if j == count_lat - 1:
                upward.append((here, (count_lon - 1 - i) * count_lat + j))
            else:
                upward.append((here, here + 1))
            if j > 0:
                downward.append((here, here - 1))
    return first, second


def lane_of(shape):
    return lax.broadcasted_iota(jnp.int32, shape, 1)


def row_of(shape):
    return lax.broadcasted_iota(jnp.int32, shape, 0)


def roll(x, shift, axis=1):
    size = x.shape[axis]
    if isinstance(shift, int):
        shift = shift % size
    return pltpu.roll(x, shift, axis)


def upwind(speed, mix):
    return jnp.maximum(speed, 0.0) + mix, jnp.minimum(speed, 0.0) - mix


def rows_kernel(NZ, NY, last, pos_ref, t_ref, s_ref, u_ref, v_ref, h_ref, m_ref, bot_ref, a_ref, b_ref):
    j = pos_ref[0]
    odd = lax.rem(j, 2) == 1
    lev = row_of((NZ, 128))
    lane = lane_of((NZ, 128))

    def message(row, inner, top):
        def at(ref, r):
            return ref[pl.ds(r, NZ, stride=NY), :]

        def sea(r):
            return (lev < bot_ref[r : r + 1, :]).astype(F32)

        w, w2 = sea(row), sea(inner)
        pe, qe = upwind(at(u_ref, row), at(h_ref, row))
        pe, qe = w * pe, w * qe
        east = jnp.where(lane < 127, roll(w, -1), 0.0)
        if top:
            pn, qn = upwind(at(v_ref, inner), at(h_ref, inner))
        else:
            pn, qn = upwind(at(v_ref, row), at(h_ref, row))
        both = w * w2
        cells, lats = [], []
        for ref in (t_ref, s_ref):
            c, c2 = w * at(ref, row), w2 * at(ref, inner)
            flux = east * (pe * c + qe * roll(c, -1))
            lat = c - flux + roll(flux, 1)
            if top:
                lat = lat + both * (pn * c2 + qn * c)
            else:
                lat = lat - both * (pn * c + qn * c2)
            cells.append(c)
            lats.append(lat)
        coupling = jnp.where(lev + 1 < bot_ref[row : row + 1, :], at(m_ref, row), 0.0)
        ends = jnp.where(lane == 127, pe, jnp.where(lane == 126, roll(qe, -1), 0.0))
        if top:
            po, qo = upwind(at(v_ref, row), at(h_ref, row))
            po, qo = w * po, w * qo
        else:
            po = qo = jnp.zeros_like(w)
        return cells + lats + [coupling, ends, po, qo]

    up = message(NY - 1, NY - 2, True)
    down = message(0, 1, False)
    for f in range(NF):
        a_ref[f * NZ : (f + 1) * NZ, :] = jnp.where(odd, up[f], down[f])
        b_ref[f * NZ : (f + 1) * NZ, :] = jnp.where(odd, down[f], up[f])
    bot_up = jnp.broadcast_to(bot_ref[NY - 1 : NY, :].astype(F32), (8, 128))
    bot_down = jnp.broadcast_to(bot_ref[0:1, :].astype(F32), (8, 128))
    a_ref[NF * NZ :, :] = jnp.where(odd, bot_up, bot_down)
    b_ref[NF * NZ :, :] = jnp.where(odd, bot_down, bot_up)

    @pl.when(j == last)
    def _():
        for r in range(0, NF * NZ + 8, 8):
            x = a_ref[r : r + 8, :]
            a_ref[r : r + 8, :] = jnp.take_along_axis(x, 127 - lane_of((8, 128)), axis=1)


def block_kernel(NZ, NY, t_ref, s_ref, u_ref, v_ref, h_ref, m_ref, bot_ref,
                 lt_ref, ls_ref, a0_ref, ae_ref, aw_ref, an_ref, as_ref, r_ref, g_ref, pk_ref):
    shape = (NY, 128)
    lane, row = lane_of(shape), row_of(shape)
    bot = bot_ref[...]
    east_in = lane < 127
    north_in = row < NY - 1

    def level(k, carry):
        above, g_above = carry[0], carry[1]
        packed = carry[2:]
        here = pl.ds(pl.multiple_of(k * NY, NY), NY)
        w = (k < bot).astype(F32)
        pe, qe = upwind(u_ref[here, :], h_ref[here, :])
        pn, qn = upwind(v_ref[here, :], h_ref[here, :])
        pe, qe = w * pe, w * qe
        we = jnp.where(east_in, roll(w, -1), 0.0)
        wn = w * jnp.where(north_in, roll(w, -1, 0), 0.0)
        pem, qem = pe * we, qe * we
        pnm, qnm = pn * wn, qn * wn
        cells, lats = [], []
        for src, dst in ((t_ref, lt_ref), (s_ref, ls_ref)):
            c = w * src[here, :]
            fe = pem * c + qem * roll(c, -1)
            fn = pnm * c + qnm * roll(c, -1, 0)
            lat = c - (fe - roll(fe, 1)) - (fn - roll(fn, 1, 0))
            dst[here, :] = lat
            cells.append(c)
            lats.append(lat)
        a0_ref[here, :] = 1.0 - pem - pnm + roll(qem, 1) + roll(qnm, 1, 0)
        ae_ref[here, :] = -qem
        aw_ref[here, :] = roll(pem, 1)
        an_ref[here, :] = -qnm
        as_ref[here, :] = roll(pnm, 1, 0)
        b = jnp.where(k + 1 < bot, m_ref[here, :], 0.0)
        r = 1.0 / (1.0 + above + b - above * g_above)
        g = b * r
        r_ref[here, :] = r
        g_ref[here, :] = g
        mine = lax.shift_right_logical(lane, 1) == k
        fields = cells + lats + [r, g, pe, qe]
        packed = tuple(jnp.where(mine, roll(x, 2 * k + 1), p) for x, p in zip(fields, packed))
        return (b, g) + packed

    zero = jnp.zeros(shape, F32)
    out = lax.fori_loop(0, NZ, level, (zero,) * 10)
    for f in range(8):
        pk_ref[f * NY : (f + 1) * NY, :] = out[2 + f]


def rim_rows(NZ, NY, last, pos_ref, ra_ref, rb_ref, t_ref, s_ref, v_ref, h_ref, bot_ref):
    j = pos_ref[0]
    odd = lax.rem(j, 2) == 1
    normal = (j != last).astype(F32)
    lev = row_of((NZ, 128))

    def south(f):
        return jnp.where(odd, rb_ref[f * NZ : (f + 1) * NZ, :], ra_ref[f * NZ : (f + 1) * NZ, :])

    def north(f):
        return jnp.where(odd, ra_ref[f * NZ : (f + 1) * NZ, :], rb_ref[f * NZ : (f + 1) * NZ, :])

    bots = jnp.where(odd, rb_ref[NF * NZ :, :], ra_ref[NF * NZ :, :])
    botn = jnp.where(odd, ra_ref[NF * NZ :, :], rb_ref[NF * NZ :, :])
    levf = lev.astype(F32)
    ws = (levf < bots[0:1, :]).astype(F32)
    wn = (levf < botn[0:1, :]).astype(F32)
    w0 = (lev < bot_ref[0:1, :]).astype(F32)
    w15 = (lev < bot_ref[NY - 1 : NY, :]).astype(F32)
    top = pl.ds(NY - 1, NZ, stride=NY)
    low = pl.ds(0, NZ, stride=NY)
    p15, q15 = upwind(v_ref[top, :], h_ref[top, :])
    p15, q15 = w15 * wn * p15, w15 * wn * q15
    als, bes = w0 * south(6), w0 * south(7)
    pf, qf = w15 * north(6), w15 * north(7)
    res = dict(bots=bots, botn=botn, als=als, bes=bes, p15=p15, q15=q15, south=south, north=north)
    fs, fn, gn = [], [], []
    for n, ref in enumerate((t_ref, s_ref)):
        c0, c15 = w0 * ref[low, :], w15 * ref[top, :]
        cs, cn = south(n), north(n)
        fs.append(als * cs + bes * c0)
        own = p15 * c15 + q15 * cn
        fn.append(own)
        gn.append(normal * own - (pf * cn + qf * c15))
    res.update(fs=fs, fn=fn, gn=gn)
    return res


def columns_kernel(NZ, NY, last, pos_ref, ra_ref, rb_ref, t_ref, s_ref, v_ref, h_ref, bot_ref, pk_ref, out_ref):
    x = rim_rows(NZ, NY, last, pos_ref, ra_ref, rb_ref, t_ref, s_ref, v_ref, h_ref, bot_ref)
    lev, lane = row_of((NZ, 128)), lane_of((NZ, 128))
    is_east, is_west = lane == 2 * lev, lane == 2 * lev + 1

    def diagonal(e, w):
        e = jnp.broadcast_to(e, (NZ, 128))
        w = jnp.broadcast_to(w, (NZ, 128))
        return jnp.sum(jnp.where(is_east, e, jnp.where(is_west, w, 0.0)), axis=0, keepdims=True)

    def ends(v):
        return diagonal(v[:, 127:128], v[:, 0:1])

    south, north = x["south"], x["north"]
    out_ref[0 : 8 * NY, :] = pk_ref[...]
    for n in range(2):
        base = (2 + n) * NY
        out_ref[base : base + 1, :] += ends(x["fs"][n])
        out_ref[base + NY - 1 : base + NY, :] -= ends(x["fn"][n])
    c = 8 * NY
    out_ref[c : c + 24, :] = jnp.zeros((24, 128), F32)
    for n in range(2):
        out_ref[c + 2 * n : c + 2 * n + 1, :] = ends(south(n))
        out_ref[c + 2 * n + 1 : c + 2 * n + 2, :] = ends(north(n))
    es, en = south(5), north(5)
    for r, e in enumerate((es, en)):
        pv = diagonal(e[:, 127:128], e[:, 0:1])
        qv = diagonal(e[:, 126:127], e[:, 1:2])
        for n in range(2):
            out_ref[c + 8 + 2 * n + r : c + 9 + 2 * n + r, :] = pv
            out_ref[c + 16 + 2 * n + r : c + 17 + 2 * n + r, :] = qv
    out_ref[c + 24 : c + 24 + NY, :] = bot_ref[...].astype(F32)
    side = row_of((8, 128))
    out_ref[c + 24 + NY : c + 32 + NY, :] = jnp.where(lax.rem(side, 2) == 0, x["bots"], x["botn"])


def ghost_rows_kernel(NZ, NY, last, pos_ref, ra_ref, rb_ref, t_ref, s_ref, v_ref, h_ref, bot_ref,
                      lt_in, ls_in, a0_in, an_in, as_in,
                      lt_ref, ls_ref, a0_ref, an_ref, as_ref, gl_ref, gr_ref, gg_ref, b_scr):
    x = rim_rows(NZ, NY, last, pos_ref, ra_ref, rb_ref, t_ref, s_ref, v_ref, h_ref, bot_ref)
    south, north = x["south"], x["north"]
    top = pl.ds(NY - 1, NZ, stride=NY)
    low = pl.ds(0, NZ, stride=NY)
    for src, dst in ((lt_in, lt_ref), (ls_in, ls_ref), (a0_in, a0_ref), (an_in, an_ref), (as_in, as_ref)):
        dst[...] = src[...]
    for n, (src, dst) in enumerate(((lt_in, lt_ref), (ls_in, ls_ref))):
        dst[low, :] = src[low, :] + x["fs"][n]
        dst[top, :] = src[top, :] - x["fn"][n]
    a0_ref[low, :] = a0_in[low, :] + x["bes"]
    a0_ref[top, :] = a0_in[top, :] - x["p15"]
    as_ref[low, :] = x["als"]
    an_ref[top, :] = -x["q15"]
    for n in range(2):
        gl_ref[pl.ds(2 * n, NZ, stride=8), :] = south(2 + n) - x["fs"][n]
        gl_ref[pl.ds(2 * n + 1, NZ, stride=8), :] = north(2 + n) + x["gn"][n]
        b_scr[pl.ds(2 * n, NZ, stride=8), :] = south(4)
        b_scr[pl.ds(2 * n + 1, NZ, stride=8), :] = north(4)
    zero = jnp.zeros((NZ, 128), F32)
    for n in range(4, 8):
        gl_ref[pl.ds(n, NZ, stride=8), :] = zero
        b_scr[pl.ds(n, NZ, stride=8), :] = zero

    def level(k, carry):
        above, g_above = carry
        here = pl.ds(pl.multiple_of(k * 8, 8), 8)
        b = b_scr[here, :]
        r = 1.0 / (1.0 + above + b - above * g_above)
        g = b * r
        gr_ref[here, :] = r
        gg_ref[here, :] = g
        return b, g

    z8 = jnp.zeros((8, 128), F32)
    lax.fori_loop(0, NZ, level, (z8, z8))


def steps_kernel(NZ, NY, rw_ref, re_ref, own_ref, lt_ref, ls_ref, a0_ref, ae_ref, aw_ref, an_ref, as_ref,
                 r_ref, g_ref, gl_ref, gr_ref, gg_ref, bot_ref, to_ref, so_ref,
                 yt, ys, ct, cs, yte, yse, re_s, ge_s, yr):
    shape = (NY, 128)
    PAD = NY + 16
    lane = lane_of(shape)
    lane8 = lane_of((8, 128))
    edge = (lane == 0) | (lane == 127)
    edge8 = (lane8 == 0) | (lane8 == 127)
    even, even8 = lax.rem(lane, 2) == 0, lax.rem(lane8, 2) == 0
    klane = lax.shift_right_logical(lane, 1).astype(F32)
    klane8 = lax.shift_right_logical(lane8, 1).astype(F32)

    def own(base, size):
        return own_ref[base : base + size, :]

    def ghost(base, size):
        ev = even if size == NY else even8
        return jnp.where(ev, roll(re_ref[base : base + size, :], -1), roll(rw_ref[base : base + size, :], 1))

    cb = 8 * NY
    bb = cb + 24

    def bottoms(base, size):
        ev = even if size == NY else even8
        sh = (size, 128)
        o, w, e = own(base, size), rw_ref[base : base + size, :], re_ref[base : base + size, :]

        def spread(x, col):
            return jnp.broadcast_to(x[:, col : col + 1], sh)

        mine = jnp.where(ev, spread(o, 127), spread(o, 0))
        theirs = jnp.where(ev, spread(e, 0), spread(w, 127))
        return mine, theirs

    bo, bg = bottoms(bb, NY)
    wo, wg = (klane < bo).astype(F32), (klane < bg).astype(F32)
    bot_edge = jnp.where(lane == 127, bg[:, 0:1], bg[:, 1:2])
    po = jnp.where(even, own(6 * NY, NY), 0.0)
    qo = jnp.where(even, own(7 * NY, NY), 0.0)
    pg = jnp.where(even, 0.0, ghost(6 * NY, NY))
    qg = jnp.where(even, 0.0, ghost(7 * NY, NY))
    alpha = wo * pg - wg * qo
    beta = wo * qg - wg * po
    corr = [alpha * ghost(n * NY, NY) + beta * own(n * NY, NY) for n in range(2)]
    glat = [ghost((2 + n) * NY, NY) - corr[n] for n in range(2)]
    gr, gg = ghost(4 * NY, NY), ghost(5 * NY, NY)

    bo8, bg8 = bottoms(bb + NY, 8)
    wo8, wg8 = (klane8 < bo8).astype(F32), (klane8 < bg8).astype(F32)
    co, cg = own(cb, 8), ghost(cb, 8)
    corner = wo8 * (ghost(cb + 8, 8) * cg + ghost(cb + 16, 8) * co) - wg8 * (own(cb + 8, 8) * co + own(cb + 16, 8) * cg)
    bot_rows = own(bb + NY, 8)
    bot = bot_ref[...]

    def down1(k, carry):
        gp, y0, y1, gep, e0, e1, ggp, yrow = carry
        here = pl.ds(pl.multiple_of(k * NY, NY), NY)
        here8 = pl.ds(pl.multiple_of(k * 8, 8), 8)
        turn = 127 - 2 * k
        y0 = lt_ref[here, :] + jnp.where(edge, roll(corr[0], turn), 0.0) + gp * y0
        y1 = ls_ref[here, :] + jnp.where(edge, roll(corr[1], turn), 0.0) + gp * y1
        e0 = roll(glat[0], turn) + gep * e0
        e1 = roll(glat[1], turn) + gep * e1
        yrow = gl_ref[here8, :] + jnp.where(edge8, roll(corner, turn), 0.0) + ggp * yrow
        yt[here, :] = y0
        ys[here, :] = y1
        yte[here, :] = e0
        yse[here, :] = e1
        yr[here8, :] = yrow
        ge = roll(gg, turn)
        re_s[here, :] = roll(gr, turn)
        ge_s[here, :] = ge
        return g_ref[here, :], y0, y1, ge, e0, e1, gg_ref[here8, :], yrow

    z, z8 = jnp.zeros(shape, F32), jnp.zeros((8, 128), F32)
    lax.fori_loop(0, NZ, down1, (z, z, z, z, z, z, z8, z8))

    def up1(n, carry):
        x0, x1, e0, e1, xr = carry
        k = NZ - 1 - n
        here = pl.ds(pl.multiple_of(k * NY, NY), NY)
        here8 = pl.ds(pl.multiple_of(k * 8, 8), 8)
        r, g = r_ref[here, :], g_ref[here, :]
        x0 = r * yt[here, :] + g * x0
        x1 = r * ys[here, :] + g * x1
        w = k < bot
        inner = pl.ds(pl.multiple_of(k * PAD + 8, 8), NY)
        ct[inner, :] = jnp.where(w, x0, 0.0)
        cs[inner, :] = jnp.where(w, x1, 0.0)
        r, g = re_s[here, :], ge_s[here, :]
        e0 = r * yte[here, :] + g * e0
        e1 = r * yse[here, :] + g * e1
        kf = k.astype(F32)
        we = kf < bot_edge
        yte[here, :] = jnp.where(we, e0, 0.0)
        yse[here, :] = jnp.where(we, e1, 0.0)
        xr = gr_ref[here8, :] * yr[here8, :] + gg_ref[here8, :] * xr
        c = jnp.where(kf < bot_rows, xr, 0.0)
        ct[pl.ds(k * PAD + 7, 1), :] = c[0:1, :]
        ct[pl.ds(k * PAD + 8 + NY, 1), :] = c[1:2, :]
        cs[pl.ds(k * PAD + 7, 1), :] = c[2:3, :]
        cs[pl.ds(k * PAD + 8 + NY, 1), :] = c[3:4, :]
        return x0, x1, e0, e1, xr

    lax.fori_loop(0, NZ, up1, (z, z, z, z, z8))

    def down2(k, carry):
        gp, y0, y1 = carry
        here = pl.ds(pl.multiple_of(k * NY, NY), NY)
        turn = 127 - 2 * k
        al = roll(alpha, turn)
        a0 = a0_ref[here, :] + jnp.where(edge, roll(beta, turn), 0.0)
        ae = jnp.where(lane == 127, al, ae_ref[here, :])
        aw = jnp.where(lane == 0, al, aw_ref[here, :])
        an, as_ = an_ref[here, :], as_ref[here, :]

        def lateral(c_ref, e_ref):
            c = c_ref[pl.ds(k * PAD + 8, NY), :]
            rim = e_ref[here, :]
            east = jnp.where(lane == 127, rim, roll(c, -1))
            west = jnp.where(lane == 0, rim, roll(c, 1))
            return (
                a0 * c + ae * east + aw * west
                + an * c_ref[pl.ds(k * PAD + 9, NY), :] + as_ * c_ref[pl.ds(k * PAD + 7, NY), :]
            )

        y0 = lateral(ct, yte) + gp * y0
        y1 = lateral(cs, yse) + gp * y1
        yt[here, :] = y0
        ys[here, :] = y1
        return g_ref[here, :], y0, y1

    lax.fori_loop(0, NZ, down2, (z, z, z))

    def up2(n, carry):
        x0, x1 = carry
        k = NZ - 1 - n
        here = pl.ds(pl.multiple_of(k * NY, NY), NY)
        r, g = r_ref[here, :], g_ref[here, :]
        x0 = r * yt[here, :] + g * x0
        x1 = r * ys[here, :] + g * x1
        w = k < bot
        to_ref[here, :] = jnp.where(w, x0, 0.0)
        so_ref[here, :] = jnp.where(w, x1, 0.0)
        return x0, x1

    lax.fori_loop(0, NZ, up2, (z, z))


VM = pl.BlockSpec(memory_space=pltpu.VMEM)
SM = pl.BlockSpec(memory_space=pltpu.SMEM)


def vmem(*shape):
    return pltpu.VMEM(shape, F32)


def call(kernel, n_in, outs, scratch=(), smem=False, cost=0, keep=True):
    specs = [SM] * smem + [VM] * (n_in - smem)
    shapes = [pltpu.VMEM(o, F32) if keep else jax.ShapeDtypeStruct(o, F32) for o in outs]
    return pl.pallas_call(
        kernel,
        out_shape=shapes,
        in_specs=specs,
        out_specs=[VM] * len(outs),
        scratch_shapes=list(scratch),
        compiler_params=pltpu.CompilerParams(vmem_limit_bytes=40 << 20),
        cost_estimate=pl.CostEstimate(flops=cost, bytes_accessed=cost, transcendentals=0) if cost else None,
    )


def per_device(temp, salt, east_speed, north_speed, mixing_h, mixing_v, wet, bottom):
    NZ, NY, NX = temp.shape
    count_lat, count_lon = lax.axis_size("lat"), lax.axis_size("lon")
    last = count_lat - 1
    flat = (NZ * NY, NX)
    t, s, u, v, h, m = (a.reshape(flat) for a in (temp, salt, east_speed, north_speed, mixing_h, mixing_v))
    pos = lax.axis_index("lat").astype(jnp.int32).reshape(1)
    rows_msg = (NF * NZ + 8, NX)
    first, second = lat_routes(count_lon, count_lat)
    axes = ("lon", "lat")

    msg_a, msg_b = call(functools.partial(rows_kernel, NZ, NY, last), 8, [rows_msg] * 2, smem=True)(
        pos, t, s, u, v, h, m, bottom
    )
    ra = lax.ppermute(msg_a, axes, first)
    rb = lax.ppermute(msg_b, axes, second)
    lt, ls, a0, ae, aw, an, as_, r, g, pk = call(
        functools.partial(block_kernel, NZ, NY), 7, [flat] * 9 + [(8 * NY, NX)], cost=10_000_000
    )(t, s, u, v, h, m, bottom)
    cols_msg = (8 * NY + 24 + NY + 8, NX)
    (cols,) = call(functools.partial(columns_kernel, NZ, NY, last), 9, [cols_msg], smem=True)(
        pos, ra, rb, t, s, v, h, bottom, pk
    )
    from_west = lax.ppermute(cols, "lon", [(i, (i + 1) % count_lon) for i in range(count_lon)])
    from_east = lax.ppermute(cols, "lon", [((i + 1) % count_lon, i) for i in range(count_lon)])
    ghost = (NZ * 8, NX)
    lt, ls, a0, an, as_, gl, gr, gg = call(
        functools.partial(ghost_rows_kernel, NZ, NY, last), 13, [flat] * 5 + [ghost] * 3,
        scratch=[vmem(*ghost)], smem=True, cost=10_000_000,
    )(pos, ra, rb, t, s, v, h, bottom, lt, ls, a0, an, as_)
    pad = (NZ * (NY + 16), NX)
    out = call(
        functools.partial(steps_kernel, NZ, NY), 16, [flat] * 2,
        scratch=[vmem(*flat), vmem(*flat), vmem(*pad), vmem(*pad)] + [vmem(*flat)] * 4 + [vmem(*ghost)], keep=False,
    )(from_west, from_east, cols, lt, ls, a0, ae, aw, an, as_, r, g, gl, gr, gg, bottom)
    return tuple(o.reshape(temp.shape) for o in out)


def solution(mesh):
    field = P(None, "lat", "lon")
    return jax.shard_map(
        per_device,
        mesh=mesh,
        in_specs=(field,) * 7 + (P("lat", "lon"),),
        out_specs=(field, field),
        check_vma=False,
    )
```

profile of v0, /device:TPU:30, one launch (start us, length us, event | category | flops | bytes accessed | tf_op | source)
XLA Modules:
  0.0 47.4 jit_solution(17197647392682090031)
XLA Ops:
  0.6 0.0 copy-start.11
  0.6 0.7 %copy-done.11 = s32[16,128]{1,0:T(8,128)S(1)} copy-done((s32[16,128]{1,0:T(8,128)S(1)}, s32[16,128]{1,0:T(8,128)}, u32[]{:S(2)}) %copy-start.11) | copy-done | bytes 8216
  1.3 0.0 copy-start
  1.3 1.0 %copy-done = f32[48,16,128]{2,1,0:T(8,128)S(1)} copy-done((f32[48,16,128]{2,1,0:T(8,128)S(1)}, f32[48,16,128]{2,1,0:T(8,128)}, u32[]{:S(2)}) %copy-start) | copy-done | bytes 393240
  2.3 0.0 copy-start.2
  2.3 1.0 %copy-done.2 = f32[48,16,128]{2,1,0:T(8,128)S(1)} copy-done((f32[48,16,128]{2,1,0:T(8,128)S(1)}, f32[48,16,128]{2,1,0:T(8,128)}, u32[]{:S(2)}) %copy-start.2) | copy-done | bytes 393240
  3.3 0.0 copy-start.4
  3.3 1.0 %copy-done.4 = f32[48,16,128]{2,1,0:T(8,128)S(1)} copy-done((f32[48,16,128]{2,1,0:T(8,128)S(1)}, f32[48,16,128]{2,1,0:T(8,128)}, u32[]{:S(2)}) %copy-start.4) | copy-done | bytes 393240
  4.3 0.0 copy-start.6
  4.3 1.0 %copy-done.6 = f32[48,16,128]{2,1,0:T(8,128)S(1)} copy-done((f32[48,16,128]{2,1,0:T(8,128)S(1)}, f32[48,16,128]{2,1,0:T(8,128)}, u32[]{:S(2)}) %copy-start.6) | copy-done | bytes 393240
  5.3 0.0 copy-start.8
  5.3 1.0 %copy-done.8 = f32[48,16,128]{2,1,0:T(8,128)S(1)} copy-done((f32[48,16,128]{2,1,0:T(8,128)S(1)}, f32[48,16,128]{2,1,0:T(8,128)}, u32[]{:S(2)}) %copy-start.8) | copy-done | bytes 393240
  6.3 0.0 copy-start.9
  6.3 1.0 %copy-done.9 = f32[48,16,128]{2,1,0:T(8,128)S(1)} copy-done((f32[48,16,128]{2,1,0:T(8,128)S(1)}, f32[48,16,128]{2,1,0:T(8,128)}, u32[]{:S(2)}) %copy-start.9) | copy-done | bytes 393240
  7.3 0.0 copy-start.1
  7.3 0.0 copy-start.3
  7.3 0.0 copy-start.5
  7.3 0.0 copy-start.7
  7.3 0.0 copy-start.10
  7.3 0.3 shard_map.86
  7.6 2.3 %collective-permute-start = (f32[392,128]{1,0:T(8,128)S(1)}, f32[392,128]{1,0:T(8,128)S(1)}, u32[]{:S(2)}, u32[]{:S(2)}) collective-permute-start(f32[392,128]{1,0:T(8,128)S(1)} %get-tuple-element.24), channel_id=1, source_target_pairs={{1,2},{2,1},{3,4},{4,3},{5,6},{6,5},{7,8},{8,7},{9,10},{10,9},{11,... | collective-permute-start | bytes 602120 | tf_op jit(solution)/shard_map/ppermute | solution.py:457
  9.9 6.2 %collective-permute-start.1 = (f32[392,128]{1,0:T(8,128)S(1)}, f32[392,128]{1,0:T(8,128)S(1)}, u32[]{:S(2)}, u32[]{:S(2)}) collective-permute-start(f32[392,128]{1,0:T(8,128)S(1)} %get-tuple-element.25), channel_id=1, source_target_pairs={{0,1},{1,0},{2,3},{3,2},{4,5},{5,4},{6,7},{7,6},{8,9},{9,8},{10,11... | collective-permute-start | bytes 602120 | tf_op jit(solution)/shard_map/ppermute | solution.py:458
  16.1 0.0 copy-done.1
  16.1 0.0 copy-done.3
  16.1 0.0 copy-done.5
  16.1 0.0 copy-done.7
  16.1 0.0 copy-done.10
  16.1 10.5 %shard_map.87 = (f32[768,128]{1,0:T(8,128)S(1)}, f32[768,128]{1,0:T(8,128)S(1)}, f32[768,128]{1,0:T(8,128)S(1)}, f32[768,128]{1,0:T(8,128)S(1)}, f32[768,128]{1,...) custom-call(f32[768,128]{1,0:T(8,128)S(1)} %bitcast.10, ...), custom_call_target="tpu_custom_call" | custom-call | flops 10000000 | bytes 10000000 | tf_op jit(solution)/shard_map/pallas_call | solution.py:459
  26.6 0.0 collective-permute-done.ra_ref
  26.6 0.0 collective-permute-done.1.rb_ref
  26.7 0.3 shard_map.88.own_ref
  27.0 3.5 %collective-permute-start.2 = (f32[176,128]{1,0:T(8,128)S(1)}, f32[176,128]{1,0:T(8,128)S(1)}, u32[]{:S(2)}, u32[]{:S(2)}) collective-permute-start(f32[176,128]{1,0:T(8,128)S(1)} %shard_map.88.own_ref), channel_id=1, source_target_pairs={{0,16},{16,32},{32,48},{48,64},{64,80},{80,96},{96,112},{112,128},... | collective-permute-start | bytes 270344 | tf_op jit(solution)/shard_map/ppermute | solution.py:466
  30.5 0.1 collective-permute-start.3
  30.6 0.9 %shard_map.89 = (f32[768,128]{1,0:T(8,128)S(1)}, f32[768,128]{1,0:T(8,128)S(1)}, f32[768,128]{1,0:T(8,128)S(1)}, f32[768,128]{1,0:T(8,128)S(1)}, f32[768,128]{1,...) custom-call(s32[1]{0:T(128)} %bitcast.pos_ref, ...), custom_call_target="tpu_custom_call" | custom-call | flops 10000000 | bytes 10000000 | tf_op jit(solution)/shard_map/pallas_call | solution.py:469
  31.5 1.7 %collective-permute-done.2.rw_ref = f32[176,128]{1,0:T(8,128)S(1)} collective-permute-done((f32[176,128]{1,0:T(8,128)S(1)}, f32[176,128]{1,0:T(8,128)S(1)}, u32[]{:S(2)}, u32[]{:S(2)}) %collective-permute-start.2) | collective-permute-done | bytes 90144 | tf_op jit(solution)/shard_map/ppermute | solution.py:466
  33.1 4.3 %collective-permute-done.3.re_ref = f32[176,128]{1,0:T(8,128)S(1)} collective-permute-done((f32[176,128]{1,0:T(8,128)S(1)}, f32[176,128]{1,0:T(8,128)S(1)}, u32[]{:S(2)}, u32[]{:S(2)}) %collective-permute-start.3) | collective-permute-done | bytes 90144 | tf_op jit(solution)/shard_map/ppermute | solution.py:467
  37.5 10.0 %shard_map.90 = (f32[768,128]{1,0:T(8,128)}, f32[768,128]{1,0:T(8,128)}) custom-call(f32[176,128]{1,0:T(8,128)S(1)} %collective-permute-done.2.rw_ref, f32[176,128]{1,0:T(8,128)S(1)} %collective-permute-done.3.re_ref, f32[176,128]{1,0:T(8,128)S(1)} %shard_map.88.own_ref, f32[768,128]{1,0:T(8,128)S(1)} %get-tuple-element.32.lt_ref, ...), custom_call_target="tpu_custom_call" | custom-call | tf_op jit(solution)/shard_map/pallas_call | solution.py:474
Async XLA Ops:
  0.6 0.7 %copy-start.11 = (s32[16,128]{1,0:T(8,128)S(1)}, s32[16,128]{1,0:T(8,128)}, u32[]{:S(2)}) copy-start(s32[16,128]{1,0:T(8,128)} %bot_ref.9) | copy-start | bytes 24580
  1.3 1.0 %copy-start = (f32[48,16,128]{2,1,0:T(8,128)S(1)}, f32[48,16,128]{2,1,0:T(8,128)}, u32[]{:S(2)}) copy-start(f32[48,16,128]{2,1,0:T(8,128)} %param.8) | copy-start | bytes 1179652
  2.3 1.0 %copy-start.2 = (f32[48,16,128]{2,1,0:T(8,128)S(1)}, f32[48,16,128]{2,1,0:T(8,128)}, u32[]{:S(2)}) copy-start(f32[48,16,128]{2,1,0:T(8,128)} %param.9) | copy-start | bytes 1179652
  3.3 1.0 %copy-start.4 = (f32[48,16,128]{2,1,0:T(8,128)S(1)}, f32[48,16,128]{2,1,0:T(8,128)}, u32[]{:S(2)}) copy-start(f32[48,16,128]{2,1,0:T(8,128)} %param.11) | copy-start | bytes 1179652
  4.3 1.0 %copy-start.6 = (f32[48,16,128]{2,1,0:T(8,128)S(1)}, f32[48,16,128]{2,1,0:T(8,128)}, u32[]{:S(2)}) copy-start(f32[48,16,128]{2,1,0:T(8,128)} %param.12) | copy-start | bytes 1179652
  5.3 1.0 %copy-start.8 = (f32[48,16,128]{2,1,0:T(8,128)S(1)}, f32[48,16,128]{2,1,0:T(8,128)}, u32[]{:S(2)}) copy-start(f32[48,16,128]{2,1,0:T(8,128)} %param.10) | copy-start | bytes 1179652
  6.3 1.0 %copy-start.9 = (f32[48,16,128]{2,1,0:T(8,128)S(1)}, f32[48,16,128]{2,1,0:T(8,128)}, u32[]{:S(2)}) copy-start(f32[48,16,128]{2,1,0:T(8,128)} %param.13) | copy-start | bytes 1179652
  7.3 8.8 %copy-start.1 = (f32[48,16,128]{2,1,0:T(8,128)S(1)}, f32[48,16,128]{2,1,0:T(8,128)}, u32[]{:S(2)}) copy-start(f32[48,16,128]{2,1,0:T(8,128)} %param.8) | copy-start | bytes 1179652
  7.3 8.8 %copy-start.3 = (f32[48,16,128]{2,1,0:T(8,128)S(1)}, f32[48,16,128]{2,1,0:T(8,128)}, u32[]{:S(2)}) copy-start(f32[48,16,128]{2,1,0:T(8,128)} %param.9) | copy-start | bytes 1179652
  7.3 8.8 %copy-start.5 = (f32[48,16,128]{2,1,0:T(8,128)S(1)}, f32[48,16,128]{2,1,0:T(8,128)}, u32[]{:S(2)}) copy-start(f32[48,16,128]{2,1,0:T(8,128)} %param.11) | copy-start | bytes 1179652
  7.3 8.8 %copy-start.7 = (f32[48,16,128]{2,1,0:T(8,128)S(1)}, f32[48,16,128]{2,1,0:T(8,128)}, u32[]{:S(2)}) copy-start(f32[48,16,128]{2,1,0:T(8,128)} %param.12) | copy-start | bytes 1179652
  7.3 8.8 %copy-start.10 = (f32[48,16,128]{2,1,0:T(8,128)S(1)}, f32[48,16,128]{2,1,0:T(8,128)}, u32[]{:S(2)}) copy-start(f32[48,16,128]{2,1,0:T(8,128)} %param.13) | copy-start | bytes 1179652
  7.6 19.0 %collective-permute-start = (f32[392,128]{1,0:T(8,128)S(1)}, f32[392,128]{1,0:T(8,128)S(1)}, u32[]{:S(2)}, u32[]{:S(2)}) collective-permute-start(f32[392,128]{1,0:T(8,128)S(1)} %get-tuple-element.24), channel_id=1, source_target_pairs={{1,2},{2,1},{3,4},{4,3},{5,6},{6,5},{7,8},{8,7},{9,10},{10,9},{11,... | collective-permute-start | bytes 602120 | tf_op jit(solution)/shard_map/ppermute | solution.py:457
  9.9 16.7 %collective-permute-start.1 = (f32[392,128]{1,0:T(8,128)S(1)}, f32[392,128]{1,0:T(8,128)S(1)}, u32[]{:S(2)}, u32[]{:S(2)}) collective-permute-start(f32[392,128]{1,0:T(8,128)S(1)} %get-tuple-element.25), channel_id=1, source_target_pairs={{0,1},{1,0},{2,3},{3,2},{4,5},{5,4},{6,7},{7,6},{8,9},{9,8},{10,11... | collective-permute-start | bytes 602120 | tf_op jit(solution)/shard_map/ppermute | solution.py:458
  27.0 6.1 %collective-permute-start.2 = (f32[176,128]{1,0:T(8,128)S(1)}, f32[176,128]{1,0:T(8,128)S(1)}, u32[]{:S(2)}, u32[]{:S(2)}) collective-permute-start(f32[176,128]{1,0:T(8,128)S(1)} %shard_map.88.own_ref), channel_id=1, source_target_pairs={{0,16},{16,32},{32,48},{48,64},{64,80},{80,96},{96,112},{112,128},... | collective-permute-start | bytes 270344 | tf_op jit(solution)/shard_map/ppermute | solution.py:466
  30.5 6.9 %collective-permute-start.3 = (f32[176,128]{1,0:T(8,128)S(1)}, f32[176,128]{1,0:T(8,128)S(1)}, u32[]{:S(2)}, u32[]{:S(2)}) collective-permute-start(f32[176,128]{1,0:T(8,128)S(1)} %shard_map.88.own_ref), channel_id=1, source_target_pairs={{16,0},{32,16},{48,32},{64,48},{80,64},{96,80},{112,96},{128,112},... | collective-permute-start | bytes 270344 | tf_op jit(solution)/shard_map/ppermute | solution.py:467
where the time goes:
time: 47.8 us; the launch traced here: 47.4 us
  Pallas kernels  21.9 us (46%)
  starting transfers between devices  12.1 us (25%)
  local copies, waits for them, and re-layouts  6.68 us (14%)
  waiting for transfers between devices  5.99 us (13%)
  between operations  0.72 us (2%)
    pallas_call x1, Pallas kernels, per_device(): call(functools.partial(block_kernel, NZ, NY), 7, [flat] * 9 + [(8 * NY, N...  10.5 us
    pallas_call x1, Pallas kernels, per_device(): call(functools.partial(steps_kernel, NZ, NY), 16, [flat] * 2, scratch=[vm...  9.95 us
    unnamed x24, local copies, waits for them, and re-layouts  6.68 us
    ppermute x1, starting transfers between devices, per_device(): rb = lax.ppermute(msg_b, axes, second)  6.19 us
    ppermute x1, waiting for transfers between devices, per_device(): lax.ppermute(cols, 'lon', [((i + 1) % count_lon, i) for i in range(count_...  4.33 us
    ppermute x1, starting transfers between devices, per_device(): lax.ppermute(cols, 'lon', [(i, (i + 1) % count_lon) for i in range(count_...  3.54 us
    ppermute x1, starting transfers between devices, per_device(): ra = lax.ppermute(msg_a, axes, first)  2.31 us
    ppermute x1, waiting for transfers between devices, per_device(): lax.ppermute(cols, 'lon', [(i, (i + 1) % count_lon) for i in range(count_...  1.66 us
  transfers between devices with their start and end apart: 4, of which 2 were waited for; matrix products, arithmetic and copies ran while one was open for 0% of the time, Pallas kernels for 24%

commit v1 on v0

--- a/solution.py
+++ b/solution.py
@@ -41,11 +41,32 @@
     return pltpu.roll(x, shift, axis)
 
 
+def in_turn(jobs, apart):
+    running, waiting, step = [], list(jobs), 0
+    while running or waiting:
+        if waiting and step % apart == 0:
+            running.append(waiting.pop(0))
+        running = [job for job in running if next(job, "end") != "end"]
+        step += 1
+
+
 def upwind(speed, mix):
     return jnp.maximum(speed, 0.0) + mix, jnp.minimum(speed, 0.0) - mix
 
 
-def rows_kernel(NZ, NY, last, pos_ref, t_ref, s_ref, u_ref, v_ref, h_ref, m_ref, bot_ref, a_ref, b_ref):
+def rows_kernel(NZ, NY, last, pos_ref, *refs):
+    sources, (a_ref, b_ref), kept, sems = refs[:7], refs[7:9], refs[9:16], refs[16]
+    t_ref, s_ref, u_ref, v_ref, h_ref, m_ref, bot_ref = kept
+    size = NZ * NY
+    copies = []
+    for n in (6, 0, 1, 2, 4, 3, 5):
+        there = kept[n] if n == 6 else kept[n].at[pl.ds(0, size)]
+        copies.append(pltpu.make_async_copy(sources[n], there, sems.at[n]))
+        copies[-1].start()
+    for n in range(6):
+        kept[n][size:, :] = jnp.zeros((8, 128), F32)
+    for copy in copies:
+        copy.wait()
     j = pos_ref[0]
     odd = lax.rem(j, 2) == 1
     lev = row_of((NZ, 128))
@@ -105,53 +126,77 @@
 
 
 def block_kernel(NZ, NY, t_ref, s_ref, u_ref, v_ref, h_ref, m_ref, bot_ref,
-                 lt_ref, ls_ref, a0_ref, ae_ref, aw_ref, an_ref, as_ref, r_ref, g_ref, pk_ref):
+                 lt_ref, ls_ref, pe_ref, qe_ref, pn_ref, qn_ref, r_ref, g_ref, pk_ref):
     shape = (NY, 128)
     lane, row = lane_of(shape), row_of(shape)
     bot = bot_ref[...]
-    east_in = lane < 127
-    north_in = row < NY - 1
-
-    def level(k, carry):
-        above, g_above = carry[0], carry[1]
-        packed = carry[2:]
-        here = pl.ds(pl.multiple_of(k * NY, NY), NY)
-        w = (k < bot).astype(F32)
-        pe, qe = upwind(u_ref[here, :], h_ref[here, :])
-        pn, qn = upwind(v_ref[here, :], h_ref[here, :])
-        pe, qe = w * pe, w * qe
-        we = jnp.where(east_in, roll(w, -1), 0.0)
-        wn = w * jnp.where(north_in, roll(w, -1, 0), 0.0)
-        pem, qem = pe * we, qe * we
-        pnm, qnm = pn * wn, qn * wn
-        cells, lats = [], []
-        for src, dst in ((t_ref, lt_ref), (s_ref, ls_ref)):
-            c = w * src[here, :]
-            fe = pem * c + qem * roll(c, -1)
-            fn = pnm * c + qnm * roll(c, -1, 0)
-            lat = c - (fe - roll(fe, 1)) - (fn - roll(fn, 1, 0))
-            dst[here, :] = lat
-            cells.append(c)
-            lats.append(lat)
-        a0_ref[here, :] = 1.0 - pem - pnm + roll(qem, 1) + roll(qnm, 1, 0)
-        ae_ref[here, :] = -qem
-        aw_ref[here, :] = roll(pem, 1)
-        an_ref[here, :] = -qnm
-        as_ref[here, :] = roll(pnm, 1, 0)
+    bot_e = jnp.where(lane < 127, roll(bot, -1), 0)
+    bot_n = jnp.where(row < NY - 1, roll(bot, -1, 0), 0)
+    pair = lax.shift_right_logical(lane, 1)
+    zero = jnp.zeros(shape, F32)
+    pn_ref[0:8, :] = jnp.zeros((8, 128), F32)
+    qn_ref[0:8, :] = jnp.zeros((8, 128), F32)
+    packed = [zero] * 8
+    chain = [zero, zero]
+
+    def level(k):
+        here = pl.ds(k * NY, NY)
+        next_row = pl.ds(k * NY + 1, NY)
+        sea, sea_e, sea_n = k < bot, k < bot_e, k < bot_n
+        cells = [jnp.where(sea, src[here, :], 0.0) for src in (t_ref, s_ref)]
+        easts = [roll(c, -1) for c in cells]
+        yield
+        yield
+        yield
+        yield
+        yield
+        h = h_ref[here, :]
+        pe, qe = upwind(u_ref[here, :], h)
+        pn, qn = upwind(v_ref[here, :], h)
+        pe, qe = jnp.where(sea, pe, 0.0), jnp.where(sea, qe, 0.0)
+        both_n = sea & sea_n
+        pem, qem = jnp.where(sea_e, pe, 0.0), jnp.where(sea_e, qe, 0.0)
+        pnm, qnm = jnp.where(both_n, pn, 0.0), jnp.where(both_n, qn, 0.0)
+        pe_ref[here, :] = pem
+        qe_ref[here, :] = qem
+        pn_ref[pl.ds(k * NY + 8, NY), :] = pnm
+        qn_ref[pl.ds(k * NY + 8, NY), :] = qnm
+        parts, wests, souths = [], [], []
+        for src, c, ce in zip((t_ref, s_ref), cells, easts):
+            cn = jnp.where(sea_n, src[next_row, :], 0.0)
+            fe = pem * c + qem * ce
+            fn = pnm * c + qnm * cn
+            parts.append(c - fe - fn)
+            wests.append(roll(fe, 1))
+            souths.append(roll(fn, 1, 0))
         b = jnp.where(k + 1 < bot, m_ref[here, :], 0.0)
-        r = 1.0 / (1.0 + above + b - above * g_above)
+        above, g = chain
+        r = 1.0 / (1.0 + above + b - above * g)
         g = b * r
+        chain[:] = b, g
         r_ref[here, :] = r
         g_ref[here, :] = g
-        mine = lax.shift_right_logical(lane, 1) == k
-        fields = cells + lats + [r, g, pe, qe]
-        packed = tuple(jnp.where(mine, roll(x, 2 * k + 1), p) for x, p in zip(fields, packed))
-        return (b, g) + packed
-
-    zero = jnp.zeros(shape, F32)
-    out = lax.fori_loop(0, NZ, level, (zero,) * 10)
+        first = [roll(x, 2 * k + 1) for x in cells + [r, g, pe, qe]]
+        yield
+        yield
+        yield
+        yield
+        yield
+        lats = [x + y + z for x, y, z in zip(parts, wests, souths)]
+        lt_ref[here, :] = lats[0]
+        ls_ref[here, :] = lats[1]
+        moved = first[:2] + [roll(x, 2 * k + 1) for x in lats] + first[2:]
+        yield
+        yield
+        yield
+        yield
+        yield
+        mine = pair == k
+        packed[:] = [jnp.where(mine, x, p) for x, p in zip(moved, packed)]
+
+    in_turn([level(k) for k in range(NZ)], 1)
     for f in range(8):
-        pk_ref[f * NY : (f + 1) * NY, :] = out[2 + f]
+        pk_ref[f * NY : (f + 1) * NY, :] = packed[f]
 
 
 def rim_rows(NZ, NY, last, pos_ref, ra_ref, rb_ref, t_ref, s_ref, v_ref, h_ref, bot_ref):
@@ -229,21 +274,12 @@
 
 
 def ghost_rows_kernel(NZ, NY, last, pos_ref, ra_ref, rb_ref, t_ref, s_ref, v_ref, h_ref, bot_ref,
-                      lt_in, ls_in, a0_in, an_in, as_in,
-                      lt_ref, ls_ref, a0_ref, an_ref, as_ref, gl_ref, gr_ref, gg_ref, b_scr):
+                      lt_in, ls_in, pe_ref, qe_ref, pn_ref, qn_ref,
+                      lt_ref, ls_ref, a0_ref, ae_ref, aw_ref, an_ref, as_ref, gl_ref, gr_ref, gg_ref, b_scr):
     x = rim_rows(NZ, NY, last, pos_ref, ra_ref, rb_ref, t_ref, s_ref, v_ref, h_ref, bot_ref)
     south, north = x["south"], x["north"]
     top = pl.ds(NY - 1, NZ, stride=NY)
     low = pl.ds(0, NZ, stride=NY)
-    for src, dst in ((lt_in, lt_ref), (ls_in, ls_ref), (a0_in, a0_ref), (an_in, an_ref), (as_in, as_ref)):
-        dst[...] = src[...]
-    for n, (src, dst) in enumerate(((lt_in, lt_ref), (ls_in, ls_ref))):
-        dst[low, :] = src[low, :] + x["fs"][n]
-        dst[top, :] = src[top, :] - x["fn"][n]
-    a0_ref[low, :] = a0_in[low, :] + x["bes"]
-    a0_ref[top, :] = a0_in[top, :] - x["p15"]
-    as_ref[low, :] = x["als"]
-    an_ref[top, :] = -x["q15"]
     for n in range(2):
         gl_ref[pl.ds(2 * n, NZ, stride=8), :] = south(2 + n) - x["fs"][n]
         gl_ref[pl.ds(2 * n + 1, NZ, stride=8), :] = north(2 + n) + x["gn"][n]
@@ -253,24 +289,37 @@
     for n in range(4, 8):
         gl_ref[pl.ds(n, NZ, stride=8), :] = zero
         b_scr[pl.ds(n, NZ, stride=8), :] = zero
-
-    def level(k, carry):
-        above, g_above = carry
-        here = pl.ds(pl.multiple_of(k * 8, 8), 8)
-        b = b_scr[here, :]
-        r = 1.0 / (1.0 + above + b - above * g_above)
+    above = g = jnp.zeros((8, 128), F32)
+    for k in range(NZ):
+        here, here8 = pl.ds(k * NY, NY), pl.ds(k * 8, 8)
+        b = b_scr[here8, :]
+        r = 1.0 / (1.0 + above + b - above * g)
         g = b * r
-        gr_ref[here, :] = r
-        gg_ref[here, :] = g
-        return b, g
-
-    z8 = jnp.zeros((8, 128), F32)
-    lax.fori_loop(0, NZ, level, (z8, z8))
+        above = b
+        gr_ref[here8, :] = r
+        gg_ref[here8, :] = g
+        lt_ref[here, :] = lt_in[here, :]
+        ls_ref[here, :] = ls_in[here, :]
+        pe, qe = pe_ref[here, :], qe_ref[here, :]
+        pn, qn = pn_ref[pl.ds(k * NY + 8, NY), :], qn_ref[pl.ds(k * NY + 8, NY), :]
+        ps, qs = pn_ref[pl.ds(k * NY + 7, NY), :], qn_ref[pl.ds(k * NY + 7, NY), :]
+        a0_ref[here, :] = 1.0 - (pe - roll(qe, 1)) - (pn - qs)
+        ae_ref[here, :] = -qe
+        aw_ref[here, :] = roll(pe, 1)
+        an_ref[here, :] = -qn
+        as_ref[here, :] = ps
+    for n, ref in enumerate((lt_ref, ls_ref)):
+        ref[low, :] = ref[low, :] + x["fs"][n]
+        ref[top, :] = ref[top, :] - x["fn"][n]
+    a0_ref[low, :] = a0_ref[low, :] + x["bes"]
+    a0_ref[top, :] = a0_ref[top, :] - x["p15"]
+    as_ref[low, :] = x["als"]
+    an_ref[top, :] = -x["q15"]
 
 
 def steps_kernel(NZ, NY, rw_ref, re_ref, own_ref, lt_ref, ls_ref, a0_ref, ae_ref, aw_ref, an_ref, as_ref,
                  r_ref, g_ref, gl_ref, gr_ref, gg_ref, bot_ref, to_ref, so_ref,
-                 yt, ys, ct, cs, yte, yse, re_s, ge_s, yr):
+                 yt, ys, ct, cs, yte, yse, re_s, ge_s, yr, xt, xs, sems):
     shape = (NY, 128)
     PAD = NY + 16
     lane = lane_of(shape)
@@ -323,10 +372,11 @@
     bot_rows = own(bb + NY, 8)
     bot = bot_ref[...]
 
-    def down1(k, carry):
-        gp, y0, y1, gep, e0, e1, ggp, yrow = carry
-        here = pl.ds(pl.multiple_of(k * NY, NY), NY)
-        here8 = pl.ds(pl.multiple_of(k * 8, 8), 8)
+    z, z8 = jnp.zeros(shape, F32), jnp.zeros((8, 128), F32)
+    y0 = y1 = e0 = e1 = gp = gep = z
+    yrow = ggp = z8
+    for k in range(NZ):
+        here, here8 = pl.ds(k * NY, NY), pl.ds(k * 8, 8)
         turn = 127 - 2 * k
         y0 = lt_ref[here, :] + jnp.where(edge, roll(corr[0], turn), 0.0) + gp * y0
         y1 = ls_ref[here, :] + jnp.where(edge, roll(corr[1], turn), 0.0) + gp * y1
@@ -338,102 +388,97 @@
         yte[here, :] = e0
         yse[here, :] = e1
         yr[here8, :] = yrow
-        ge = roll(gg, turn)
+        gep = roll(gg, turn)
         re_s[here, :] = roll(gr, turn)
-        ge_s[here, :] = ge
-        return g_ref[here, :], y0, y1, ge, e0, e1, gg_ref[here8, :], yrow
-
-    z, z8 = jnp.zeros(shape, F32), jnp.zeros((8, 128), F32)
-    lax.fori_loop(0, NZ, down1, (z, z, z, z, z, z, z8, z8))
-
-    def up1(n, carry):
-        x0, x1, e0, e1, xr = carry
-        k = NZ - 1 - n
-        here = pl.ds(pl.multiple_of(k * NY, NY), NY)
-        here8 = pl.ds(pl.multiple_of(k * 8, 8), 8)
+        ge_s[here, :] = gep
+        gp, ggp = g_ref[here, :], gg_ref[here8, :]
+
+    x0 = x1 = e0 = e1 = z
+    xr = z8
+    for k in reversed(range(NZ)):
+        here, here8 = pl.ds(k * NY, NY), pl.ds(k * 8, 8)
+        inner = pl.ds(k * PAD + 8, NY)
         r, g = r_ref[here, :], g_ref[here, :]
         x0 = r * yt[here, :] + g * x0
         x1 = r * ys[here, :] + g * x1
         w = k < bot
-        inner = pl.ds(pl.multiple_of(k * PAD + 8, 8), NY)
         ct[inner, :] = jnp.where(w, x0, 0.0)
         cs[inner, :] = jnp.where(w, x1, 0.0)
         r, g = re_s[here, :], ge_s[here, :]
         e0 = r * yte[here, :] + g * e0
         e1 = r * yse[here, :] + g * e1
-        kf = k.astype(F32)
-        we = kf < bot_edge
+        we = k < bot_edge
         yte[here, :] = jnp.where(we, e0, 0.0)
         yse[here, :] = jnp.where(we, e1, 0.0)
         xr = gr_ref[here8, :] * yr[here8, :] + gg_ref[here8, :] * xr
-        c = jnp.where(kf < bot_rows, xr, 0.0)
+        c = jnp.where(k < bot_rows, xr, 0.0)
         ct[pl.ds(k * PAD + 7, 1), :] = c[0:1, :]
         ct[pl.ds(k * PAD + 8 + NY, 1), :] = c[1:2, :]
         cs[pl.ds(k * PAD + 7, 1), :] = c[2:3, :]
         cs[pl.ds(k * PAD + 8 + NY, 1), :] = c[3:4, :]
-        return x0, x1, e0, e1, xr
-
-    lax.fori_loop(0, NZ, up1, (z, z, z, z, z8))
-
-    def down2(k, carry):
-        gp, y0, y1 = carry
-        here = pl.ds(pl.multiple_of(k * NY, NY), NY)
+
+    gp = y0 = y1 = z
+    for k in range(NZ):
+        here = pl.ds(k * NY, NY)
         turn = 127 - 2 * k
         al = roll(alpha, turn)
         a0 = a0_ref[here, :] + jnp.where(edge, roll(beta, turn), 0.0)
         ae = jnp.where(lane == 127, al, ae_ref[here, :])
         aw = jnp.where(lane == 0, al, aw_ref[here, :])
         an, as_ = an_ref[here, :], as_ref[here, :]
-
-        def lateral(c_ref, e_ref):
+        ys_new = []
+        for c_ref, e_ref in ((ct, yte), (cs, yse)):
             c = c_ref[pl.ds(k * PAD + 8, NY), :]
             rim = e_ref[here, :]
             east = jnp.where(lane == 127, rim, roll(c, -1))
             west = jnp.where(lane == 0, rim, roll(c, 1))
-            return (
-                a0 * c + ae * east + aw * west
-                + an * c_ref[pl.ds(k * PAD + 9, NY), :] + as_ * c_ref[pl.ds(k * PAD + 7, NY), :]
+            ys_new.append(
+                a0 * c + (ae * east + aw * west)
+                + (an * c_ref[pl.ds(k * PAD + 9, NY), :] + as_ * c_ref[pl.ds(k * PAD + 7, NY), :])
             )
-
-        y0 = lateral(ct, yte) + gp * y0
-        y1 = lateral(cs, yse) + gp * y1
+        y0 = ys_new[0] + gp * y0
+        y1 = ys_new[1] + gp * y1
         yt[here, :] = y0
         ys[here, :] = y1
-        return g_ref[here, :], y0, y1
-
-    lax.fori_loop(0, NZ, down2, (z, z, z))
-
-    def up2(n, carry):
-        x0, x1 = carry
-        k = NZ - 1 - n
-        here = pl.ds(pl.multiple_of(k * NY, NY), NY)
+        gp = g_ref[here, :]
+
+    x0 = x1 = z
+    part = max(NZ // CHUNKS, 1)
+    copies = []
+    for k in reversed(range(NZ)):
+        here = pl.ds(k * NY, NY)
         r, g = r_ref[here, :], g_ref[here, :]
         x0 = r * yt[here, :] + g * x0
         x1 = r * ys[here, :] + g * x1
         w = k < bot
-        to_ref[here, :] = jnp.where(w, x0, 0.0)
-        so_ref[here, :] = jnp.where(w, x1, 0.0)
-        return x0, x1
-
-    lax.fori_loop(0, NZ, up2, (z, z))
+        xt[here, :] = jnp.where(w, x0, 0.0)
+        xs[here, :] = jnp.where(w, x1, 0.0)
+        if k % part == 0:
+            chunk = pl.ds(k * NY, part * NY)
+            for n, (src, dst) in enumerate(((xt, to_ref), (xs, so_ref))):
+                copy = pltpu.make_async_copy(src.at[chunk], dst.at[chunk], sems.at[n, k // part])
+                copy.start()
+                copies.append(copy)
+    for copy in copies:
+        copy.wait()
 
 
 VM = pl.BlockSpec(memory_space=pltpu.VMEM)
 SM = pl.BlockSpec(memory_space=pltpu.SMEM)
+HB = pl.BlockSpec(memory_space=pltpu.HBM)
+CHUNKS = 4
 
 
 def vmem(*shape):
     return pltpu.VMEM(shape, F32)
 
 
-def call(kernel, n_in, outs, scratch=(), smem=False, cost=0, keep=True):
-    specs = [SM] * smem + [VM] * (n_in - smem)
-    shapes = [pltpu.VMEM(o, F32) if keep else jax.ShapeDtypeStruct(o, F32) for o in outs]
+def call(kernel, ins, outs, out_specs=None, scratch=(), cost=0):
     return pl.pallas_call(
         kernel,
-        out_shape=shapes,
-        in_specs=specs,
-        out_specs=[VM] * len(outs),
+        out_shape=outs,
+        in_specs=ins,
+        out_specs=out_specs or [VM] * len(outs),
         scratch_shapes=list(scratch),
         compiler_params=pltpu.CompilerParams(vmem_limit_bytes=40 << 20),
         cost_estimate=pl.CostEstimate(flops=cost, bytes_accessed=cost, transcendentals=0) if cost else None,
@@ -444,37 +489,41 @@
     NZ, NY, NX = temp.shape
     count_lat, count_lon = lax.axis_size("lat"), lax.axis_size("lon")
     last = count_lat - 1
-    flat = (NZ * NY, NX)
-    t, s, u, v, h, m = (a.reshape(flat) for a in (temp, salt, east_speed, north_speed, mixing_h, mixing_v))
+    size = NZ * NY
+    flat = vmem(size, NX)
+    fields = [a.reshape(size, NX) for a in (temp, salt, east_speed, north_speed, mixing_h, mixing_v)]
     pos = lax.axis_index("lat").astype(jnp.int32).reshape(1)
-    rows_msg = (NF * NZ + 8, NX)
     first, second = lat_routes(count_lon, count_lat)
     axes = ("lon", "lat")
 
-    msg_a, msg_b = call(functools.partial(rows_kernel, NZ, NY, last), 8, [rows_msg] * 2, smem=True)(
-        pos, t, s, u, v, h, m, bottom
-    )
+    msg_a, msg_b, t, s, u, v, h, m, bot = call(
+        functools.partial(rows_kernel, NZ, NY, last),
+        [SM] + [HB] * 7,
+        [vmem(NF * NZ + 8, NX)] * 2 + [vmem(size + 8, NX)] * 6 + [pltpu.VMEM((NY, NX), jnp.int32)],
+        scratch=[pltpu.SemaphoreType.DMA((7,))],
+    )(pos, *[pltpu.with_memory_space_constraint(a, pltpu.HBM) for a in fields], pltpu.with_memory_space_constraint(bottom, pltpu.HBM))
     ra = lax.ppermute(msg_a, axes, first)
     rb = lax.ppermute(msg_b, axes, second)
-    lt, ls, a0, ae, aw, an, as_, r, g, pk = call(
-        functools.partial(block_kernel, NZ, NY), 7, [flat] * 9 + [(8 * NY, NX)], cost=10_000_000
-    )(t, s, u, v, h, m, bottom)
-    cols_msg = (8 * NY + 24 + NY + 8, NX)
-    (cols,) = call(functools.partial(columns_kernel, NZ, NY, last), 9, [cols_msg], smem=True)(
-        pos, ra, rb, t, s, v, h, bottom, pk
-    )
+    lt, ls, pe, qe, pn, qn, r, g, pk = call(
+        functools.partial(block_kernel, NZ, NY), [VM] * 7,
+        [flat] * 4 + [vmem(size + 8, NX)] * 2 + [flat] * 2 + [vmem(8 * NY, NX)], cost=10_000_000,
+    )(t, s, u, v, h, m, bot)
+    (cols,) = call(
+        functools.partial(columns_kernel, NZ, NY, last), [SM] + [VM] * 8, [vmem(8 * NY + 24 + NY + 8, NX)]
+    )(pos, ra, rb, t, s, v, h, bot, pk)
     from_west = lax.ppermute(cols, "lon", [(i, (i + 1) % count_lon) for i in range(count_lon)])
     from_east = lax.ppermute(cols, "lon", [((i + 1) % count_lon, i) for i in range(count_lon)])
-    ghost = (NZ * 8, NX)
-    lt, ls, a0, an, as_, gl, gr, gg = call(
-        functools.partial(ghost_rows_kernel, NZ, NY, last), 13, [flat] * 5 + [ghost] * 3,
-        scratch=[vmem(*ghost)], smem=True, cost=10_000_000,
-    )(pos, ra, rb, t, s, v, h, bottom, lt, ls, a0, an, as_)
-    pad = (NZ * (NY + 16), NX)
+    ghost = vmem(NZ * 8, NX)
+    lt, ls, a0, ae, aw, an, as_, gl, gr, gg = call(
+        functools.partial(ghost_rows_kernel, NZ, NY, last), [SM] + [VM] * 13, [flat] * 7 + [ghost] * 3,
+        scratch=[ghost], cost=10_000_000,
+    )(pos, ra, rb, t, s, v, h, bot, lt, ls, pe, qe, pn, qn)
+    pad = vmem(NZ * (NY + 16), NX)
     out = call(
-        functools.partial(steps_kernel, NZ, NY), 16, [flat] * 2,
-        scratch=[vmem(*flat), vmem(*flat), vmem(*pad), vmem(*pad)] + [vmem(*flat)] * 4 + [vmem(*ghost)], keep=False,
-    )(from_west, from_east, cols, lt, ls, a0, ae, aw, an, as_, r, g, gl, gr, gg, bottom)
+        functools.partial(steps_kernel, NZ, NY), [VM] * 16,
+        [jax.ShapeDtypeStruct((size, NX), F32)] * 2, out_specs=[HB] * 2,
+        scratch=[flat] * 2 + [pad] * 2 + [flat] * 4 + [ghost] + [flat] * 2 + [pltpu.SemaphoreType.DMA((2, CHUNKS))],
+    )(from_west, from_east, cols, lt, ls, a0, ae, aw, an, as_, r, g, gl, gr, gg, bot)
     return tuple(o.reshape(temp.shape) for o in out)
 
 

time: 47.8 us -> 29.1 us (0.61)
  the two profiles are of different devices: /device:TPU:30 before, /device:TPU:127 now
where the time goes in v1:
time: 29.1 us; the launch traced here: 28.9 us
  waiting for transfers between devices  11.3 us (39%)
  starting transfers between devices  9.46 us (33%)
  Pallas kernels  7.47 us (26%)
  between operations  0.68 us (2%)
    ppermute x1, starting transfers between devices, per_device(): ra = lax.ppermute(msg_a, axes, first)  5.6 us
    ppermute x1, waiting for transfers between devices, per_device(): lax.ppermute(cols, 'lon', [((i + 1) % count_lon, i) for i in range(count_...  5.43 us
    ppermute x1, waiting for transfers between devices, per_device(): ra = lax.ppermute(msg_a, axes, first)  5.06 us
    ppermute x1, starting transfers between devices, per_device(): lax.ppermute(cols, 'lon', [(i, (i + 1) % count_lon) for i in range(count_...  3.77 us
    pallas_call x1, Pallas kernels, per_device(): call(functools.partial(steps_kernel, NZ, NY), [VM] * 16, [jax.ShapeDtypeS...  2.88 us
    pallas_call x1, Pallas kernels, per_device(): call(functools.partial(rows_kernel, NZ, NY, last), [SM] + [HB] * 7, [vmem...  2.06 us
    pallas_call x1, Pallas kernels, per_device(): call(functools.partial(block_kernel, NZ, NY), [VM] * 7, [flat] * 4 + [vme...  1.44 us
    ppermute x1, waiting for transfers between devices, per_device(): lax.ppermute(cols, 'lon', [(i, (i + 1) % count_lon) for i in range(count_...  0.8 us
  transfers between devices with their start and end apart: 4, of which 3 were waited for; matrix products, arithmetic and copies ran while one was open for 0% of the time, Pallas kernels for 8%

profile of v1, /device:TPU:127, one launch (start us, length us, event | category | flops | bytes accessed | tf_op | source)
XLA Modules:
  0.0 28.9 jit_solution(8536853514928268869)
XLA Ops:
  0.6 2.1 %shard_map.86 = (f32[392,128]{1,0:T(8,128)S(1)}, f32[392,128]{1,0:T(8,128)S(1)}, f32[776,128]{1,0:T(8,128)S(1)}, f32[776,128]{1,0:T(8,128)S(1)}, f32[776,128]{1,...) custom-call(s32[1]{0:T(128)} %bitcast.pos_ref, ...), custom_call_target="tpu_custom_call" | custom-call | tf_op jit(solution)/shard_map/pallas_call | solution.py:499
  2.7 5.6 %collective-permute-start = (f32[392,128]{1,0:T(8,128)S(1)}, f32[392,128]{1,0:T(8,128)S(1)}, u32[]{:S(2)}, u32[]{:S(2)}) collective-permute-start(f32[392,128]{1,0:T(8,128)S(1)} %get-tuple-element.32), channel_id=1, source_target_pairs={{1,2},{2,1},{3,4},{4,3},{5,6},{6,5},{7,8},{8,7},{9,10},{10,9},{11,... | collective-permute-start | bytes 602120 | tf_op jit(solution)/shard_map/ppermute | solution.py:505
  8.3 0.1 collective-permute-start.1
  8.4 1.4 %shard_map.87 = (f32[768,128]{1,0:T(8,128)S(1)}, f32[768,128]{1,0:T(8,128)S(1)}, f32[768,128]{1,0:T(8,128)S(1)}, f32[768,128]{1,0:T(8,128)S(1)}, f32[776,128]{1,...) custom-call(f32[776,128]{1,0:T(8,128)S(1)} %get-tuple-element.34.t_r, ...), custom_call_target="tpu_custom_call" | custom-call | flops 10000000 | bytes 10000000 | tf_op jit(solution)/shard_map/pallas_call | solution.py:507
  9.9 5.1 %collective-permute-done.ra_ref = f32[392,128]{1,0:T(8,128)S(1)} collective-permute-done((f32[392,128]{1,0:T(8,128)S(1)}, f32[392,128]{1,0:T(8,128)S(1)}, u32[]{:S(2)}, u32[]{:S(2)}) %collective-permute-start) | collective-permute-done | bytes 200736 | tf_op jit(solution)/shard_map/ppermute | solution.py:505
  14.9 0.0 collective-permute-done.1.rb_ref
  14.9 0.3 %shard_map.88.own_ref = f32[176,128]{1,0:T(8,128)S(1)} custom-call(s32[1]{0:T(128)} %bitcast.pos_ref, f32[392,128]{1,0:T(8,128)S(1)} %collective-permute-done.ra_ref, f32[392,128]{1,0:T(8,128)S(1)} %collective-permute-done.1.rb_ref, f32[776,128]{1,0:T(8,128)S(1)} %get-tuple-element.34.t_ref, f32[776,128]{1,0:T(8,128)S(1)} %get-tuple-element.35.s_ref, ...), custom_call_target="tpu_custom_call" | custom-call | tf_op jit(solution)/shard_map/pallas_call | solution.py:511
  15.3 3.8 %collective-permute-start.2 = (f32[176,128]{1,0:T(8,128)S(1)}, f32[176,128]{1,0:T(8,128)S(1)}, u32[]{:S(2)}, u32[]{:S(2)}) collective-permute-start(f32[176,128]{1,0:T(8,128)S(1)} %shard_map.88.own_ref), channel_id=1, source_target_pairs={{0,16},{16,32},{32,48},{48,64},{64,80},{80,96},{96,112},{112,128},... | collective-permute-start | bytes 270344 | tf_op jit(solution)/shard_map/ppermute | solution.py:514
  19.0 0.0 collective-permute-start.3
  19.0 0.8 %shard_map.89 = (f32[768,128]{1,0:T(8,128)S(1)}, f32[768,128]{1,0:T(8,128)S(1)}, f32[768,128]{1,0:T(8,128)S(1)}, f32[768,128]{1,0:T(8,128)S(1)}, f32[768,128]{1,...) custom-call(s32[1]{0:T(128)} %bitcast.pos_ref, ...), custom_call_target="tpu_custom_call" | custom-call | flops 10000000 | bytes 10000000 | tf_op jit(solution)/shard_map/pallas_call | solution.py:517
  19.8 0.8 %collective-permute-done.2.rw_ref = f32[176,128]{1,0:T(8,128)S(1)} collective-permute-done((f32[176,128]{1,0:T(8,128)S(1)}, f32[176,128]{1,0:T(8,128)S(1)}, u32[]{:S(2)}, u32[]{:S(2)}) %collective-permute-start.2) | collective-permute-done | bytes 90144 | tf_op jit(solution)/shard_map/ppermute | solution.py:514
  20.6 5.4 %collective-permute-done.3.re_ref = f32[176,128]{1,0:T(8,128)S(1)} collective-permute-done((f32[176,128]{1,0:T(8,128)S(1)}, f32[176,128]{1,0:T(8,128)S(1)}, u32[]{:S(2)}, u32[]{:S(2)}) %collective-permute-start.3) | collective-permute-done | bytes 90144 | tf_op jit(solution)/shard_map/ppermute | solution.py:515
  26.0 2.9 %shard_map.90 = (f32[768,128]{1,0:T(8,128)}, f32[768,128]{1,0:T(8,128)}) custom-call(f32[176,128]{1,0:T(8,128)S(1)} %collective-permute-done.2.rw_ref, f32[176,128]{1,0:T(8,128)S(1)} %collective-permute-done.3.re_ref, f32[176,128]{1,0:T(8,128)S(1)} %shard_map.88.own_ref, f32[768,128]{1,0:T(8,128)S(1)} %get-tuple-element.48.lt_ref, ...), custom_call_target="tpu_custom_call" | custom-call | tf_op jit(solution)/shard_map/pallas_call | solution.py:522
Async XLA Ops:
  2.7 12.2 %collective-permute-start = (f32[392,128]{1,0:T(8,128)S(1)}, f32[392,128]{1,0:T(8,128)S(1)}, u32[]{:S(2)}, u32[]{:S(2)}) collective-permute-start(f32[392,128]{1,0:T(8,128)S(1)} %get-tuple-element.32), channel_id=1, source_target_pairs={{1,2},{2,1},{3,4},{4,3},{5,6},{6,5},{7,8},{8,7},{9,10},{10,9},{11,... | collective-permute-start | bytes 602120 | tf_op jit(solution)/shard_map/ppermute | solution.py:505
  8.3 6.6 %collective-permute-start.1 = (f32[392,128]{1,0:T(8,128)S(1)}, f32[392,128]{1,0:T(8,128)S(1)}, u32[]{:S(2)}, u32[]{:S(2)}) collective-permute-start(f32[392,128]{1,0:T(8,128)S(1)} %get-tuple-element.33), channel_id=1, source_target_pairs={{0,1},{1,0},{2,3},{3,2},{4,5},{5,4},{6,7},{7,6},{8,9},{9,8},{10,11... | collective-permute-start | bytes 602120 | tf_op jit(solution)/shard_map/ppermute | solution.py:506
  15.3 5.3 %collective-permute-start.2 = (f32[176,128]{1,0:T(8,128)S(1)}, f32[176,128]{1,0:T(8,128)S(1)}, u32[]{:S(2)}, u32[]{:S(2)}) collective-permute-start(f32[176,128]{1,0:T(8,128)S(1)} %shard_map.88.own_ref), channel_id=1, source_target_pairs={{0,16},{16,32},{32,48},{48,64},{64,80},{80,96},{96,112},{112,128},... | collective-permute-start | bytes 270344 | tf_op jit(solution)/shard_map/ppermute | solution.py:514
  19.0 7.0 %collective-permute-start.3 = (f32[176,128]{1,0:T(8,128)S(1)}, f32[176,128]{1,0:T(8,128)S(1)}, u32[]{:S(2)}, u32[]{:S(2)}) collective-permute-start(f32[176,128]{1,0:T(8,128)S(1)} %shard_map.88.own_ref), channel_id=1, source_target_pairs={{16,0},{32,16},{48,32},{64,48},{80,64},{96,80},{112,96},{128,112},... | collective-permute-start | bytes 270344 | tf_op jit(solution)/shard_map/ppermute | solution.py:515

commit v2 on v1

--- a/solution.py
+++ b/solution.py
@@ -8,7 +8,8 @@
 from jax.sharding import PartitionSpec as P
 
 F32 = jnp.float32
-NF = 8
+NF = 7
+NFIRST = 4
 
 
 def lat_routes(count_lon, count_lat):
@@ -41,6 +42,14 @@
     return pltpu.roll(x, shift, axis)
 
 
+def diagonal(NZ, even, odd):
+    lev, lane = row_of((NZ, 128)), lane_of((NZ, 128))
+    even = jnp.broadcast_to(even, (NZ, 128))
+    odd = jnp.broadcast_to(odd, (NZ, 128))
+    picked = jnp.where(lane == 2 * lev, even, jnp.where(lane == 2 * lev + 1, odd, 0.0))
+    return jnp.sum(picked, axis=0, keepdims=True)
+
+
 def in_turn(jobs, apart):
     running, waiting, step = [], list(jobs), 0
     while running or waiting:
@@ -55,7 +64,7 @@
 
 
 def rows_kernel(NZ, NY, last, pos_ref, *refs):
-    sources, (a_ref, b_ref), kept, sems = refs[:7], refs[7:9], refs[9:16], refs[16]
+    sources, (a_ref, a2_ref, b_ref, tails_ref), kept, sems = refs[:7], refs[7:11], refs[11:18], refs[18]
     t_ref, s_ref, u_ref, v_ref, h_ref, m_ref, bot_ref = kept
     size = NZ * NY
     copies = []
@@ -67,7 +76,7 @@
         kept[n][size:, :] = jnp.zeros((8, 128), F32)
     for copy in copies:
         copy.wait()
-    j = pos_ref[0]
+    j = lax.rem(pos_ref[0], last + 1)
     odd = lax.rem(j, 2) == 1
     lev = row_of((NZ, 128))
     lane = lane_of((NZ, 128))
@@ -100,29 +109,43 @@
             cells.append(c)
             lats.append(lat)
         coupling = jnp.where(lev + 1 < bot_ref[row : row + 1, :], at(m_ref, row), 0.0)
-        ends = jnp.where(lane == 127, pe, jnp.where(lane == 126, roll(qe, -1), 0.0))
         if top:
             po, qo = upwind(at(v_ref, row), at(h_ref, row))
             po, qo = w * po, w * qo
         else:
             po = qo = jnp.zeros_like(w)
-        return cells + lats + [coupling, ends, po, qo]
+        row8 = row_of((8, 128))
+        tail = jnp.zeros((8, 128), F32)
+        lines = [bot_ref[row : row + 1, :].astype(F32), diagonal(NZ, pe[:, 127:128], qe[:, 127:128])]
+        lines += [diagonal(NZ, x[:, 127:128], x[:, 0:1]) for x in (cells + [po, qo] if top else cells)]
+        for n, line in enumerate(lines):
+            tail = jnp.where(row8 == n, jnp.broadcast_to(line, (8, 128)), tail)
+        return cells + lats + [coupling, po, qo, tail]
 
     up = message(NY - 1, NY - 2, True)
     down = message(0, 1, False)
     for f in range(NF):
-        a_ref[f * NZ : (f + 1) * NZ, :] = jnp.where(odd, up[f], down[f])
+        value = jnp.where(odd, up[f], down[f])
+        if f < NFIRST:
+            a_ref[f * NZ : (f + 1) * NZ, :] = value
+        else:
+            a2_ref[(f - NFIRST) * NZ : (f - NFIRST + 1) * NZ, :] = value
         b_ref[f * NZ : (f + 1) * NZ, :] = jnp.where(odd, down[f], up[f])
-    bot_up = jnp.broadcast_to(bot_ref[NY - 1 : NY, :].astype(F32), (8, 128))
-    bot_down = jnp.broadcast_to(bot_ref[0:1, :].astype(F32), (8, 128))
-    a_ref[NF * NZ :, :] = jnp.where(odd, bot_up, bot_down)
-    b_ref[NF * NZ :, :] = jnp.where(odd, bot_down, bot_up)
+    a_ref[NFIRST * NZ :, :] = jnp.where(odd, up[NF], down[NF])
+    b_ref[NF * NZ :, :] = jnp.where(odd, down[NF], up[NF])
+    tails_ref[0:8, :] = up[NF]
+    tails_ref[8:16, :] = down[NF]
 
     @pl.when(j == last)
     def _():
-        for r in range(0, NF * NZ + 8, 8):
-            x = a_ref[r : r + 8, :]
-            a_ref[r : r + 8, :] = jnp.take_along_axis(x, 127 - lane_of((8, 128)), axis=1)
+        row8, lane8 = row_of((8, 128)), lane_of((8, 128))
+        for ref, size in ((a_ref, NFIRST * NZ), (a2_ref, (NF - NFIRST) * NZ)):
+            for r in range(0, size, 8):
+                ref[r : r + 8, :] = jnp.take_along_axis(ref[r : r + 8, :], 127 - lane8, axis=1)
+        x = a_ref[NFIRST * NZ :, :]
+        swapped = jnp.where(lax.rem(lane8, 2) == 0, roll(x, -1), roll(x, 1))
+        flipped = jnp.take_along_axis(x, 127 - lane8, axis=1)
+        a_ref[NFIRST * NZ :, :] = jnp.where(row8 == 0, flipped, jnp.where(row8 == 1, x, swapped))
 
 
 def block_kernel(NZ, NY, t_ref, s_ref, u_ref, v_ref, h_ref, m_ref, bot_ref,
@@ -199,20 +222,24 @@
         pk_ref[f * NY : (f + 1) * NY, :] = packed[f]
 
 
-def rim_rows(NZ, NY, last, pos_ref, ra_ref, rb_ref, t_ref, s_ref, v_ref, h_ref, bot_ref):
-    j = pos_ref[0]
+def rim_rows(NZ, NY, last, pos_ref, ra_ref, ra2_ref, rb_ref, t_ref, s_ref, v_ref, h_ref, bot_ref):
+    j = lax.rem(pos_ref[0], last + 1)
     odd = lax.rem(j, 2) == 1
     normal = (j != last).astype(F32)
     lev = row_of((NZ, 128))
 
+    def chips(f):
+        ref, f = (ra_ref, f) if f < NFIRST else (ra2_ref, f - NFIRST)
+        return ref[f * NZ : (f + 1) * NZ, :]
+
     def south(f):
-        return jnp.where(odd, rb_ref[f * NZ : (f + 1) * NZ, :], ra_ref[f * NZ : (f + 1) * NZ, :])
+        return jnp.where(odd, rb_ref[f * NZ : (f + 1) * NZ, :], chips(f))
 
     def north(f):
-        return jnp.where(odd, ra_ref[f * NZ : (f + 1) * NZ, :], rb_ref[f * NZ : (f + 1) * NZ, :])
-
-    bots = jnp.where(odd, rb_ref[NF * NZ :, :], ra_ref[NF * NZ :, :])
-    botn = jnp.where(odd, ra_ref[NF * NZ :, :], rb_ref[NF * NZ :, :])
+        return jnp.where(odd, chips(f), rb_ref[f * NZ : (f + 1) * NZ, :])
+
+    bots = jnp.where(odd, rb_ref[NF * NZ :, :], ra_ref[NFIRST * NZ :, :])
+    botn = jnp.where(odd, ra_ref[NFIRST * NZ :, :], rb_ref[NF * NZ :, :])
     levf = lev.astype(F32)
     ws = (levf < bots[0:1, :]).astype(F32)
     wn = (levf < botn[0:1, :]).astype(F32)
@@ -222,9 +249,9 @@
     low = pl.ds(0, NZ, stride=NY)
     p15, q15 = upwind(v_ref[top, :], h_ref[top, :])
     p15, q15 = w15 * wn * p15, w15 * wn * q15
-    als, bes = w0 * south(6), w0 * south(7)
-    pf, qf = w15 * north(6), w15 * north(7)
-    res = dict(bots=bots, botn=botn, als=als, bes=bes, p15=p15, q15=q15, south=south, north=north)
+    als, bes = w0 * south(5), w0 * south(6)
+    pf, qf = w15 * north(5), w15 * north(6)
+    res = dict(als=als, bes=bes, p15=p15, q15=q15, south=south, north=north)
     fs, fn, gn = [], [], []
     for n, ref in enumerate((t_ref, s_ref)):
         c0, c15 = w0 * ref[low, :], w15 * ref[top, :]
@@ -237,46 +264,73 @@
     return res
 
 
-def columns_kernel(NZ, NY, last, pos_ref, ra_ref, rb_ref, t_ref, s_ref, v_ref, h_ref, bot_ref, pk_ref, out_ref):
-    x = rim_rows(NZ, NY, last, pos_ref, ra_ref, rb_ref, t_ref, s_ref, v_ref, h_ref, bot_ref)
-    lev, lane = row_of((NZ, 128)), lane_of((NZ, 128))
-    is_east, is_west = lane == 2 * lev, lane == 2 * lev + 1
-
-    def diagonal(e, w):
-        e = jnp.broadcast_to(e, (NZ, 128))
-        w = jnp.broadcast_to(w, (NZ, 128))
-        return jnp.sum(jnp.where(is_east, e, jnp.where(is_west, w, 0.0)), axis=0, keepdims=True)
-
-    def ends(v):
-        return diagonal(v[:, 127:128], v[:, 0:1])
-
-    south, north = x["south"], x["north"]
-    out_ref[0 : 8 * NY, :] = pk_ref[...]
+def columns_kernel(NZ, NY, last, pos_ref, ra_ref, rb_ref, tails_ref, bot_ref, pk_ref, a_ref, b_ref, own_ref):
+    j = lax.rem(pos_ref[0], last + 1)
+    odd, fold = lax.rem(j, 2) == 1, j == last
+    odd_lon = lax.rem(lax.div(pos_ref[0], last + 1), 2) == 1
+    urgent, other = ra_ref[NFIRST * NZ :, :], rb_ref[NF * NZ :, :]
+    south, north = jnp.where(odd, other, urgent), jnp.where(odd, urgent, other)
+    bot = bot_ref[...].astype(F32)
+    up, down = tails_ref[0:8, :], tails_ref[8:16, :]
+    lane1 = lane_of((1, 128))
+    klane = lax.shift_right_logical(lane1, 1).astype(F32)
+
+    def sea(levels):
+        east, west = jnp.broadcast_to(levels[:, 127:128], (1, 128)), jnp.broadcast_to(levels[:, 0:1], (1, 128))
+        return (klane < jnp.where(lax.rem(lane1, 2) == 0, east, west)).astype(F32)
+
+    w0, wn = sea(bot[0:1, :]), sea(north[0:1, :])
+    row8, lane8 = row_of((8, 128)), lane_of((8, 128))
+    even8 = lax.rem(lane8, 2) == 0
+    packed = [pk_ref[f * NY : (f + 1) * NY, :] for f in range(8)]
+    row = row_of((NY, 128))
     for n in range(2):
-        base = (2 + n) * NY
-        out_ref[base : base + 1, :] += ends(x["fs"][n])
-        out_ref[base + NY - 1 : base + NY, :] -= ends(x["fn"][n])
-    c = 8 * NY
-    out_ref[c : c + 24, :] = jnp.zeros((24, 128), F32)
-    for n in range(2):
-        out_ref[c + 2 * n : c + 2 * n + 1, :] = ends(south(n))
-        out_ref[c + 2 * n + 1 : c + 2 * n + 2, :] = ends(north(n))
-    es, en = south(5), north(5)
-    for r, e in enumerate((es, en)):
-        pv = diagonal(e[:, 127:128], e[:, 0:1])
-        qv = diagonal(e[:, 126:127], e[:, 1:2])
-        for n in range(2):
-            out_ref[c + 8 + 2 * n + r : c + 9 + 2 * n + r, :] = pv
-            out_ref[c + 16 + 2 * n + r : c + 17 + 2 * n + r, :] = qv
-    out_ref[c + 24 : c + 24 + NY, :] = bot_ref[...].astype(F32)
-    side = row_of((8, 128))
-    out_ref[c + 24 + NY : c + 32 + NY, :] = jnp.where(lax.rem(side, 2) == 0, x["bots"], x["botn"])
-
-
-def ghost_rows_kernel(NZ, NY, last, pos_ref, ra_ref, rb_ref, t_ref, s_ref, v_ref, h_ref, bot_ref,
+        c = slice(2 + n, 3 + n)
+        fs = w0 * (south[4:5, :] * south[c, :] + south[5:6, :] * down[c, :])
+        fn = wn * (up[4:5, :] * up[c, :] + up[5:6, :] * north[c, :])
+        packed[2 + n] = packed[2 + n] + jnp.where(row == 0, fs, jnp.where(row == NY - 1, -fn, 0.0))
+
+    def four(a, b, c, d):
+        return jnp.where(row8 == 0, a, jnp.where(row8 == 1, b, jnp.where(row8 == 2, c, d)))
+
+    cells = four(south[2:3, :], north[2:3, :], south[3:4, :], north[3:4, :])
+    es, en = south[1:2, :], north[1:2, :]
+    e = jnp.where(lax.rem(row8, 2) == 0, jnp.broadcast_to(es, (8, 128)), jnp.broadcast_to(en, (8, 128)))
+    mirrored = fold & (lax.rem(row8, 2) == 1)
+    p = jnp.where(mirrored, jnp.where(even8, 0.0, roll(e, 1)), jnp.where(even8, e, 0.0))
+    q = jnp.where(mirrored, jnp.where(even8, 0.0, e), jnp.where(even8, roll(e, -1), 0.0))
+    bots, botn = jnp.broadcast_to(south[0:1, :], (8, 128)), jnp.broadcast_to(north[0:1, :], (8, 128))
+    levels = jnp.where(lax.rem(row8, 2) == 0, bots, botn)
+    for n, f in enumerate((0, 1, 6, 7)):
+        own_ref[n * NY : (n + 1) * NY, :] = packed[f]
+    base = 4 * NY
+    own_ref[base : base + 8, :] = cells
+    own_ref[base + 8 : base + 16, :] = p
+    own_ref[base + 16 : base + 24, :] = q
+    own_ref[base + 24 : base + 32, :] = levels
+
+    lane = lane_of((NY, 128))
+    even = lax.rem(lane, 2) == 0
+    for n in range(4):
+        f1, f2 = packed[2 * n], packed[2 * n + 1]
+        to_east = jnp.where(even, f1, roll(f2, 1))
+        to_west = jnp.where(even, roll(f1, -1), f2)
+        if n == 0:
+            to_east = jnp.where(lane >= 96, bot[:, 127:128], to_east)
+            to_west = jnp.where(lane >= 96, bot[:, 0:1], to_west)
+        a_ref[n * NY : (n + 1) * NY, :] = jnp.where(odd_lon, to_west, to_east)
+        b_ref[n * NY : (n + 1) * NY, :] = jnp.where(odd_lon, to_east, to_west)
+    corner = jnp.where(row8 < 4, cells, jnp.where(row8 < 6, p, q))
+    to_east = jnp.where(lane8 >= 96, levels[:, 127:128], corner)
+    to_west = jnp.where(lane8 >= 96, levels[:, 0:1], corner)
+    a_ref[base : base + 8, :] = jnp.where(odd_lon, to_west, to_east)
+    b_ref[base : base + 8, :] = jnp.where(odd_lon, to_east, to_west)
+
+
+def ghost_rows_kernel(NZ, NY, last, pos_ref, ra_ref, ra2_ref, rb_ref, t_ref, s_ref, v_ref, h_ref, bot_ref,
                       lt_in, ls_in, pe_ref, qe_ref, pn_ref, qn_ref,
                       lt_ref, ls_ref, a0_ref, ae_ref, aw_ref, an_ref, as_ref, gl_ref, gr_ref, gg_ref, b_scr):
-    x = rim_rows(NZ, NY, last, pos_ref, ra_ref, rb_ref, t_ref, s_ref, v_ref, h_ref, bot_ref)
+    x = rim_rows(NZ, NY, last, pos_ref, ra_ref, ra2_ref, rb_ref, t_ref, s_ref, v_ref, h_ref, bot_ref)
     south, north = x["south"], x["north"]
     top = pl.ds(NY - 1, NZ, stride=NY)
     low = pl.ds(0, NZ, stride=NY)
@@ -317,7 +371,7 @@
     an_ref[top, :] = -x["q15"]
 
 
-def steps_kernel(NZ, NY, rw_ref, re_ref, own_ref, lt_ref, ls_ref, a0_ref, ae_ref, aw_ref, an_ref, as_ref,
+def steps_kernel(NZ, NY, last, pos_ref, ra_ref, rb_ref, own_ref, lt_ref, ls_ref, a0_ref, ae_ref, aw_ref, an_ref, as_ref,
                  r_ref, g_ref, gl_ref, gr_ref, gg_ref, bot_ref, to_ref, so_ref,
                  yt, ys, ct, cs, yte, yse, re_s, ge_s, yr, xt, xs, sems):
     shape = (NY, 128)
@@ -330,47 +384,53 @@
     klane = lax.shift_right_logical(lane, 1).astype(F32)
     klane8 = lax.shift_right_logical(lane8, 1).astype(F32)
 
-    def own(base, size):
-        return own_ref[base : base + size, :]
-
-    def ghost(base, size):
-        ev = even if size == NY else even8
-        return jnp.where(ev, roll(re_ref[base : base + size, :], -1), roll(rw_ref[base : base + size, :], 1))
-
-    cb = 8 * NY
-    bb = cb + 24
-
-    def bottoms(base, size):
-        ev = even if size == NY else even8
-        sh = (size, 128)
-        o, w, e = own(base, size), rw_ref[base : base + size, :], re_ref[base : base + size, :]
-
-        def spread(x, col):
-            return jnp.broadcast_to(x[:, col : col + 1], sh)
-
-        mine = jnp.where(ev, spread(o, 127), spread(o, 0))
-        theirs = jnp.where(ev, spread(e, 0), spread(w, 127))
-        return mine, theirs
-
-    bo, bg = bottoms(bb, NY)
+    odd_lon = lax.rem(lax.div(pos_ref[0], last + 1), 2) == 1
+    base = 4 * NY
+
+    def own(start, size):
+        return own_ref[start : start + size, :]
+
+    def received(start, size):
+        a, b = ra_ref[start : start + size, :], rb_ref[start : start + size, :]
+        return jnp.where(odd_lon, a, b), jnp.where(odd_lon, b, a)
+
+    def spread(x, col, size):
+        return jnp.broadcast_to(x[:, col : col + 1], (size, 128))
+
+    ghosts = []
+    for n in range(4):
+        west, east = received(n * NY, NY)
+        if n == 0:
+            bg_east, bg_west = spread(east, 96, NY), spread(west, 96, NY)
+        ghosts.append(jnp.where(even, east, roll(west, 1)))
+        ghosts.append(jnp.where(even, roll(east, -1), west))
+    west, east = received(base, 8)
+    bg8 = jnp.where(even8, spread(east, 96, 8), spread(west, 96, 8))
+    corners = jnp.where(even8, roll(east, -1), roll(west, 1))
+    bot = bot_ref[...]
+    botf = bot.astype(F32)
+    bo = jnp.where(even, spread(botf, 127, NY), spread(botf, 0, NY))
+    bg = jnp.where(even, bg_east, bg_west)
     wo, wg = (klane < bo).astype(F32), (klane < bg).astype(F32)
-    bot_edge = jnp.where(lane == 127, bg[:, 0:1], bg[:, 1:2])
-    po = jnp.where(even, own(6 * NY, NY), 0.0)
-    qo = jnp.where(even, own(7 * NY, NY), 0.0)
-    pg = jnp.where(even, 0.0, ghost(6 * NY, NY))
-    qg = jnp.where(even, 0.0, ghost(7 * NY, NY))
+    bot_edge = jnp.where(lane == 127, bg_east, bg_west)
+    po = jnp.where(even, own(2 * NY, NY), 0.0)
+    qo = jnp.where(even, own(3 * NY, NY), 0.0)
+    pg = jnp.where(even, 0.0, ghosts[6])
+    qg = jnp.where(even, 0.0, ghosts[7])
     alpha = wo * pg - wg * qo
     beta = wo * qg - wg * po
-    corr = [alpha * ghost(n * NY, NY) + beta * own(n * NY, NY) for n in range(2)]
-    glat = [ghost((2 + n) * NY, NY) - corr[n] for n in range(2)]
-    gr, gg = ghost(4 * NY, NY), ghost(5 * NY, NY)
-
-    bo8, bg8 = bottoms(bb + NY, 8)
+    corr = [alpha * ghosts[n] + beta * own(n * NY, NY) for n in range(2)]
+    glat = [ghosts[2 + n] - corr[n] for n in range(2)]
+    gr, gg = ghosts[4], ghosts[5]
+
+    bot_rows = own(base + 24, 8)
+    bo8 = jnp.where(even8, spread(bot_rows, 127, 8), spread(bot_rows, 0, 8))
     wo8, wg8 = (klane8 < bo8).astype(F32), (klane8 < bg8).astype(F32)
-    co, cg = own(cb, 8), ghost(cb, 8)
-    corner = wo8 * (ghost(cb + 8, 8) * cg + ghost(cb + 16, 8) * co) - wg8 * (own(cb + 8, 8) * co + own(cb + 16, 8) * cg)
-    bot_rows = own(bb + NY, 8)
-    bot = bot_ref[...]
+    first_two = row_of((8, 128)) < 2
+    pg8 = jnp.where(first_two, roll(corners, -4, 0), roll(corners, -2, 0))
+    qg8 = jnp.where(first_two, roll(corners, -6, 0), roll(corners, -4, 0))
+    co, po8, qo8 = own(base, 8), own(base + 8, 8), own(base + 16, 8)
+    corner = wo8 * (pg8 * corners + qg8 * co) - wg8 * (po8 * co + qo8 * corners)
 
     z, z8 = jnp.zeros(shape, F32), jnp.zeros((8, 128), F32)
     y0 = y1 = e0 = e1 = gp = gep = z
@@ -492,38 +552,42 @@
     size = NZ * NY
     flat = vmem(size, NX)
     fields = [a.reshape(size, NX) for a in (temp, salt, east_speed, north_speed, mixing_h, mixing_v)]
-    pos = lax.axis_index("lat").astype(jnp.int32).reshape(1)
+    axes = ("lon", "lat")
+    pos = lax.axis_index(axes).astype(jnp.int32).reshape(1)
     first, second = lat_routes(count_lon, count_lat)
-    axes = ("lon", "lat")
-
-    msg_a, msg_b, t, s, u, v, h, m, bot = call(
+
+    msg_a, msg_a2, msg_b, tails, t, s, u, v, h, m, bot = call(
         functools.partial(rows_kernel, NZ, NY, last),
         [SM] + [HB] * 7,
-        [vmem(NF * NZ + 8, NX)] * 2 + [vmem(size + 8, NX)] * 6 + [pltpu.VMEM((NY, NX), jnp.int32)],
+        [vmem(NFIRST * NZ + 8, NX), vmem((NF - NFIRST) * NZ, NX), vmem(NF * NZ + 8, NX), vmem(16, NX)]
+        + [vmem(size + 8, NX)] * 6 + [pltpu.VMEM((NY, NX), jnp.int32)],
         scratch=[pltpu.SemaphoreType.DMA((7,))],
     )(pos, *[pltpu.with_memory_space_constraint(a, pltpu.HBM) for a in fields], pltpu.with_memory_space_constraint(bottom, pltpu.HBM))
     ra = lax.ppermute(msg_a, axes, first)
     rb = lax.ppermute(msg_b, axes, second)
+    upward = [(x, y) for x, y in first if NFIRST < 5 or x % count_lat % 2]
+    ra2 = lax.ppermute(msg_a2, axes, upward)
     lt, ls, pe, qe, pn, qn, r, g, pk = call(
         functools.partial(block_kernel, NZ, NY), [VM] * 7,
         [flat] * 4 + [vmem(size + 8, NX)] * 2 + [flat] * 2 + [vmem(8 * NY, NX)], cost=10_000_000,
     )(t, s, u, v, h, m, bot)
-    (cols,) = call(
-        functools.partial(columns_kernel, NZ, NY, last), [SM] + [VM] * 8, [vmem(8 * NY + 24 + NY + 8, NX)]
-    )(pos, ra, rb, t, s, v, h, bot, pk)
-    from_west = lax.ppermute(cols, "lon", [(i, (i + 1) % count_lon) for i in range(count_lon)])
-    from_east = lax.ppermute(cols, "lon", [((i + 1) % count_lon, i) for i in range(count_lon)])
+    col_msg = vmem(4 * NY + 8, NX)
+    cols_a, cols_b, own = call(
+        functools.partial(columns_kernel, NZ, NY, last), [SM] + [VM] * 5, [col_msg] * 2 + [vmem(4 * NY + 32, NX)]
+    )(pos, ra, rb, tails, bot, pk)
+    ca = lax.ppermute(cols_a, "lon", [(i, i ^ 1) for i in range(count_lon)])
+    cb = lax.ppermute(cols_b, "lon", [(i, (i + 1 if i % 2 else i - 1) % count_lon) for i in range(count_lon)])
     ghost = vmem(NZ * 8, NX)
     lt, ls, a0, ae, aw, an, as_, gl, gr, gg = call(
-        functools.partial(ghost_rows_kernel, NZ, NY, last), [SM] + [VM] * 13, [flat] * 7 + [ghost] * 3,
+        functools.partial(ghost_rows_kernel, NZ, NY, last), [SM] + [VM] * 14, [flat] * 7 + [ghost] * 3,
         scratch=[ghost], cost=10_000_000,
-    )(pos, ra, rb, t, s, v, h, bot, lt, ls, pe, qe, pn, qn)
+    )(pos, ra, ra2, rb, t, s, v, h, bot, lt, ls, pe, qe, pn, qn)
     pad = vmem(NZ * (NY + 16), NX)
     out = call(
-        functools.partial(steps_kernel, NZ, NY), [VM] * 16,
+        functools.partial(steps_kernel, NZ, NY, last), [SM] + [VM] * 16,
         [jax.ShapeDtypeStruct((size, NX), F32)] * 2, out_specs=[HB] * 2,
         scratch=[flat] * 2 + [pad] * 2 + [flat] * 4 + [ghost] + [flat] * 2 + [pltpu.SemaphoreType.DMA((2, CHUNKS))],
-    )(from_west, from_east, cols, lt, ls, a0, ae, aw, an, as_, r, g, gl, gr, gg, bot)
+    )(pos, ca, cb, own, lt, ls, a0, ae, aw, an, as_, r, g, gl, gr, gg, bot)
     return tuple(o.reshape(temp.shape) for o in out)
 
 

time: 29.1 us -> 27.1 us (0.931)
  the two profiles are of different devices: /device:TPU:127 before, /device:TPU:27 now
where the time goes in v2:
time: 27.1 us; the launch traced here: 26.9 us
  starting transfers between devices  17.9 us (66%)
  Pallas kernels  7.45 us (27%)
  waiting for transfers between devices  0.83 us (3%)
  between operations  0.7 us (3%)
    ppermute x1, starting transfers between devices, per_device(): ra = lax.ppermute(msg_a, axes, first)  9.03 us
    ppermute x1, starting transfers between devices, per_device(): lax.ppermute(cols_b, 'lon', [(i, (i + 1 if i % 2 else i - 1) % count_lon)...  5.07 us
    pallas_call x1, Pallas kernels, per_device(): call(functools.partial(steps_kernel, NZ, NY, last), [SM] + [VM] * 16, [ja...  2.94 us
    pallas_call x1, Pallas kernels, per_device(): call(functools.partial(rows_kernel, NZ, NY, last), [SM] + [HB] * 7, [vmem...  2.24 us
    ppermute x1, starting transfers between devices, per_device(): ra2 = lax.ppermute(msg_a2, axes, upward)  1.92 us
    pallas_call x1, Pallas kernels, per_device(): call(functools.partial(block_kernel, NZ, NY), [VM] * 7, [flat] * 4 + [vme...  1.43 us
    ppermute x1, starting transfers between devices, per_device(): ca = lax.ppermute(cols_a, 'lon', [(i, i ^ 1) for i in range(count_lon)])  1.21 us
    ppermute x1, waiting for transfers between devices, per_device(): lax.ppermute(cols_b, 'lon', [(i, (i + 1 if i % 2 else i - 1) % count_lon)...  0.82 us
  transfers between devices with their start and end apart: 5, of which 1 were waited for; matrix products, arithmetic and copies ran while one was open for 0% of the time, Pallas kernels for 8%

profile of v2, /device:TPU:27, one launch (start us, length us, event | category | flops | bytes accessed | tf_op | source)
XLA Modules:
  0.0 26.9 jit_solution(5336045873704775346)
XLA Ops:
  0.6 2.2 %shard_map.86 = (f32[200,128]{1,0:T(8,128)S(1)}, f32[144,128]{1,0:T(8,128)S(1)}, f32[344,128]{1,0:T(8,128)S(1)}, f32[16,128]{1,0:T(8,128)S(1)}, f32[776,128]{1,0...) custom-call(s32[1]{0:T(128)} %bitcast.pos_ref, ...), custom_call_target="tpu_custom_call" | custom-call | tf_op jit(solution)/shard_map/pallas_call | solution.py:559
  2.9 0.6 %collective-permute-start.1 = (f32[344,128]{1,0:T(8,128)S(1)}, f32[344,128]{1,0:T(8,128)S(1)}, u32[]{:S(2)}, u32[]{:S(2)}) collective-permute-start(f32[344,128]{1,0:T(8,128)S(1)} %get-tuple-element.38), channel_id=1, source_target_pairs={{0,1},{1,0},{2,3},{3,2},{4,5},{5,4},{6,7},{7,6},{8,9},{9,8},{10,11... | collective-permute-start | bytes 528392 | tf_op jit(solution)/shard_map/ppermute | solution.py:567
  3.5 9.0 %collective-permute-start = (f32[200,128]{1,0:T(8,128)S(1)}, f32[200,128]{1,0:T(8,128)S(1)}, u32[]{:S(2)}, u32[]{:S(2)}) collective-permute-start(f32[200,128]{1,0:T(8,128)S(1)} %get-tuple-element.37), channel_id=1, source_target_pairs={{1,2},{2,1},{3,4},{4,3},{5,6},{6,5},{7,8},{8,7},{9,10},{10,9},{11,... | collective-permute-start | bytes 307208 | tf_op jit(solution)/shard_map/ppermute | solution.py:566
  12.6 1.9 %collective-permute-start.4 = (f32[144,128]{1,0:T(8,128)S(1)}, f32[144,128]{1,0:T(8,128)S(1)}, u32[]{:S(2)}, u32[]{:S(2)}) collective-permute-start(f32[144,128]{1,0:T(8,128)S(1)} %get-tuple-element.51), channel_id=1, source_target_pairs={{1,2},{2,1},{3,4},{4,3},{5,6},{6,5},{7,8},{8,7},{9,10},{10,9},{11,... | collective-permute-start | bytes 221192 | tf_op jit(solution)/shard_map/ppermute | solution.py:569
  14.5 1.4 %shard_map.87 = (f32[768,128]{1,0:T(8,128)S(1)}, f32[768,128]{1,0:T(8,128)S(1)}, f32[768,128]{1,0:T(8,128)S(1)}, f32[768,128]{1,0:T(8,128)S(1)}, f32[776,128]{1,...) custom-call(f32[776,128]{1,0:T(8,128)S(1)} %get-tuple-element.41.t_r, ...), custom_call_target="tpu_custom_call" | custom-call | flops 10000000 | bytes 10000000 | tf_op jit(solution)/shard_map/pallas_call | solution.py:570
  15.9 0.0 collective-permute-done.ra_ref
  15.9 0.0 collective-permute-done.1.rb_ref
  16.0 0.2 shard_map.88
  16.1 1.2 %collective-permute-start.2 = (f32[72,128]{1,0:T(8,128)S(1)}, f32[72,128]{1,0:T(8,128)S(1)}, u32[]{:S(2)}, u32[]{:S(2)}) collective-permute-start(f32[72,128]{1,0:T(8,128)S(1)} %get-tuple-element.48), channel_id=1, source_target_pairs={{0,16},{16,0},{32,48},{48,32},{64,80},{80,64},{96,112},{112,96},{1... | collective-permute-start | bytes 110600 | tf_op jit(solution)/shard_map/ppermute | solution.py:578
  17.3 5.1 %collective-permute-start.3 = (f32[72,128]{1,0:T(8,128)S(1)}, f32[72,128]{1,0:T(8,128)S(1)}, u32[]{:S(2)}, u32[]{:S(2)}) collective-permute-start(f32[72,128]{1,0:T(8,128)S(1)} %get-tuple-element.49), channel_id=1, source_target_pairs={{0,240},{16,32},{32,16},{48,64},{64,48},{80,96},{96,80},{112,128},... | collective-permute-start | bytes 110600 | tf_op jit(solution)/shard_map/ppermute | solution.py:579
  22.4 0.0 collective-permute-done.4.ra2_ref
  22.4 0.7 %shard_map.89 = (f32[768,128]{1,0:T(8,128)S(1)}, f32[768,128]{1,0:T(8,128)S(1)}, f32[768,128]{1,0:T(8,128)S(1)}, f32[768,128]{1,0:T(8,128)S(1)}, f32[768,128]{1,...) custom-call(s32[1]{0:T(128)} %bitcast.pos_ref, ...), custom_call_target="tpu_custom_call" | custom-call | flops 10000000 | bytes 10000000 | tf_op jit(solution)/shard_map/pallas_call | solution.py:581
  23.1 0.0 collective-permute-done.2.ra_ref
  23.1 0.8 %collective-permute-done.3.rb_ref = f32[72,128]{1,0:T(8,128)S(1)} collective-permute-done((f32[72,128]{1,0:T(8,128)S(1)}, f32[72,128]{1,0:T(8,128)S(1)}, u32[]{:S(2)}, u32[]{:S(2)}) %collective-permute-start.3) | collective-permute-done | bytes 36896 | tf_op jit(solution)/shard_map/ppermute | solution.py:579
  23.9 2.9 %shard_map.90 = (f32[768,128]{1,0:T(8,128)}, f32[768,128]{1,0:T(8,128)}) custom-call(s32[1]{0:T(128)} %bitcast.pos_ref, f32[72,128]{1,0:T(8,128)S(1)} %collective-permute-done.2.ra_ref, f32[72,128]{1,0:T(8,128)S(1)} %collective-permute-done.3.rb_ref, f32[96,128]{1,0:T(8,128)S(1)} %get-tuple-element.50.own_ref, f32[768,128]{1,0:T(8,128)S(1)} %get-tuple-element.58.lt_ref, ...), custom_call_target="tpu_custom_call" | custom-call | tf_op jit(solution)/shard_map/pallas_call | solution.py:586
Async XLA Ops:
  2.9 13.1 %collective-permute-start.1 = (f32[344,128]{1,0:T(8,128)S(1)}, f32[344,128]{1,0:T(8,128)S(1)}, u32[]{:S(2)}, u32[]{:S(2)}) collective-permute-start(f32[344,128]{1,0:T(8,128)S(1)} %get-tuple-element.38), channel_id=1, source_target_pairs={{0,1},{1,0},{2,3},{3,2},{4,5},{5,4},{6,7},{7,6},{8,9},{9,8},{10,11... | collective-permute-start | bytes 528392 | tf_op jit(solution)/shard_map/ppermute | solution.py:567
  3.5 12.4 %collective-permute-start = (f32[200,128]{1,0:T(8,128)S(1)}, f32[200,128]{1,0:T(8,128)S(1)}, u32[]{:S(2)}, u32[]{:S(2)}) collective-permute-start(f32[200,128]{1,0:T(8,128)S(1)} %get-tuple-element.37), channel_id=1, source_target_pairs={{1,2},{2,1},{3,4},{4,3},{5,6},{6,5},{7,8},{8,7},{9,10},{10,9},{11,... | collective-permute-start | bytes 307208 | tf_op jit(solution)/shard_map/ppermute | solution.py:566
  12.6 9.8 %collective-permute-start.4 = (f32[144,128]{1,0:T(8,128)S(1)}, f32[144,128]{1,0:T(8,128)S(1)}, u32[]{:S(2)}, u32[]{:S(2)}) collective-permute-start(f32[144,128]{1,0:T(8,128)S(1)} %get-tuple-element.51), channel_id=1, source_target_pairs={{1,2},{2,1},{3,4},{4,3},{5,6},{6,5},{7,8},{8,7},{9,10},{10,9},{11,... | collective-permute-start | bytes 221192 | tf_op jit(solution)/shard_map/ppermute | solution.py:569
  16.1 7.0 %collective-permute-start.2 = (f32[72,128]{1,0:T(8,128)S(1)}, f32[72,128]{1,0:T(8,128)S(1)}, u32[]{:S(2)}, u32[]{:S(2)}) collective-permute-start(f32[72,128]{1,0:T(8,128)S(1)} %get-tuple-element.48), channel_id=1, source_target_pairs={{0,16},{16,0},{32,48},{48,32},{64,80},{80,64},{96,112},{112,96},{1... | collective-permute-start | bytes 110600 | tf_op jit(solution)/shard_map/ppermute | solution.py:578
  17.3 6.6 %collective-permute-start.3 = (f32[72,128]{1,0:T(8,128)S(1)}, f32[72,128]{1,0:T(8,128)S(1)}, u32[]{:S(2)}, u32[]{:S(2)}) collective-permute-start(f32[72,128]{1,0:T(8,128)S(1)} %get-tuple-element.49), channel_id=1, source_target_pairs={{0,240},{16,32},{32,16},{48,64},{64,48},{80,96},{96,80},{112,128},... | collective-permute-start | bytes 110600 | tf_op jit(solution)/shard_map/ppermute | solution.py:579

commit v3 on v2

--- a/solution.py
+++ b/solution.py
@@ -48,6 +48,17 @@
     odd = jnp.broadcast_to(odd, (NZ, 128))
     picked = jnp.where(lane == 2 * lev, even, jnp.where(lane == 2 * lev + 1, odd, 0.0))
     return jnp.sum(picked, axis=0, keepdims=True)
+
+
+def inward(NZ):
+    half = NZ // 2
+    return [pair for k in range(half) for pair in ((k, 0), (NZ - 1 - k, 1))]
+
+
+def meet(top, bottom):
+    (rt, gt, yt), (rb, gb, yb) = top, bottom
+    xt, xb, d = rt * yt, rb * yb, 1.0 / (1.0 - gt * gb)
+    return (xb + gb * xt) * d, (xt + gt * xb) * d
 
 
 def in_turn(jobs, apart):
@@ -160,9 +171,12 @@
     pn_ref[0:8, :] = jnp.zeros((8, 128), F32)
     qn_ref[0:8, :] = jnp.zeros((8, 128), F32)
     packed = [zero] * 8
-    chain = [zero, zero]
-
-    def level(k):
+    chains = [[zero, zero], [zero, zero]]
+
+    def coupling(k):
+        return jnp.where(k + 1 < bot, m_ref[pl.ds(k * NY, NY), :], 0.0)
+
+    def level(k, side):
         here = pl.ds(k * NY, NY)
         next_row = pl.ds(k * NY + 1, NY)
         sea, sea_e, sea_n = k < bot, k < bot_e, k < bot_n
@@ -192,11 +206,11 @@
             parts.append(c - fe - fn)
             wests.append(roll(fe, 1))
             souths.append(roll(fn, 1, 0))
-        b = jnp.where(k + 1 < bot, m_ref[here, :], 0.0)
-        above, g = chain
-        r = 1.0 / (1.0 + above + b - above * g)
+        b = coupling(k - side)
+        behind, g = chains[side]
+        r = 1.0 / (1.0 + behind + b - behind * g)
         g = b * r
-        chain[:] = b, g
+        chains[side][:] = b, g
         r_ref[here, :] = r
         g_ref[here, :] = g
         first = [roll(x, 2 * k + 1) for x in cells + [r, g, pe, qe]]
@@ -217,7 +231,7 @@
         mine = pair == k
         packed[:] = [jnp.where(mine, x, p) for x, p in zip(moved, packed)]
 
-    in_turn([level(k) for k in range(NZ)], 1)
+    in_turn([level(*pair) for pair in inward(NZ)], 1)
     for f in range(8):
         pk_ref[f * NY : (f + 1) * NY, :] = packed[f]
 
@@ -343,13 +357,15 @@
     for n in range(4, 8):
         gl_ref[pl.ds(n, NZ, stride=8), :] = zero
         b_scr[pl.ds(n, NZ, stride=8), :] = zero
-    above = g = jnp.zeros((8, 128), F32)
-    for k in range(NZ):
+    z8 = jnp.zeros((8, 128), F32)
+    chains = [[z8, z8], [z8, z8]]
+    for k, side in inward(NZ):
         here, here8 = pl.ds(k * NY, NY), pl.ds(k * 8, 8)
-        b = b_scr[here8, :]
-        r = 1.0 / (1.0 + above + b - above * g)
+        b = b_scr[pl.ds((k - side) * 8, 8), :]
+        behind, g = chains[side]
+        r = 1.0 / (1.0 + behind + b - behind * g)
         g = b * r
-        above = b
+        chains[side][:] = b, g
         gr_ref[here8, :] = r
         gg_ref[here8, :] = g
         lt_ref[here, :] = lt_in[here, :]
@@ -433,9 +449,10 @@
     corner = wo8 * (pg8 * corners + qg8 * co) - wg8 * (po8 * co + qo8 * corners)
 
     z, z8 = jnp.zeros(shape, F32), jnp.zeros((8, 128), F32)
-    y0 = y1 = e0 = e1 = gp = gep = z
-    yrow = ggp = z8
-    for k in range(NZ):
+    state = [(z, z, z, z, z, z, z8, z8)] * 2
+    last_r = [None, None]
+    for k, side in inward(NZ):
+        y0, y1, e0, e1, gp, gep, yrow, ggp = state[side]
         here, here8 = pl.ds(k * NY, NY), pl.ds(k * 8, 8)
         turn = 127 - 2 * k
         y0 = lt_ref[here, :] + jnp.where(edge, roll(corr[0], turn), 0.0) + gp * y0
@@ -449,13 +466,20 @@
         yse[here, :] = e1
         yr[here8, :] = yrow
         gep = roll(gg, turn)
-        re_s[here, :] = roll(gr, turn)
+        rep = roll(gr, turn)
+        re_s[here, :] = rep
         ge_s[here, :] = gep
         gp, ggp = g_ref[here, :], gg_ref[here8, :]
-
-    x0 = x1 = e0 = e1 = z
-    xr = z8
-    for k in reversed(range(NZ)):
+        state[side] = y0, y1, e0, e1, gp, gep, yrow, ggp
+        if abs(2 * k + 1 - NZ) == 1:
+            last_r[side] = r_ref[here, :], rep, gr_ref[here8, :]
+
+    found = []
+    for y, r, g in ((0, 0, 4), (1, 0, 4), (2, 1, 5), (3, 1, 5), (6, 2, 7)):
+        found.append(meet(*[(last_r[side][r], state[side][g], state[side][y]) for side in range(2)]))
+    state = [tuple(x[side] for x in found) for side in range(2)]
+    for k, side in reversed(inward(NZ)):
+        x0, x1, e0, e1, xr = state[side]
         here, here8 = pl.ds(k * NY, NY), pl.ds(k * 8, 8)
         inner = pl.ds(k * PAD + 8, NY)
         r, g = r_ref[here, :], g_ref[here, :]
@@ -471,14 +495,16 @@
         yte[here, :] = jnp.where(we, e0, 0.0)
         yse[here, :] = jnp.where(we, e1, 0.0)
         xr = gr_ref[here8, :] * yr[here8, :] + gg_ref[here8, :] * xr
+        state[side] = x0, x1, e0, e1, xr
         c = jnp.where(k < bot_rows, xr, 0.0)
         ct[pl.ds(k * PAD + 7, 1), :] = c[0:1, :]
         ct[pl.ds(k * PAD + 8 + NY, 1), :] = c[1:2, :]
         cs[pl.ds(k * PAD + 7, 1), :] = c[2:3, :]
         cs[pl.ds(k * PAD + 8 + NY, 1), :] = c[3:4, :]
 
-    gp = y0 = y1 = z
-    for k in range(NZ):
+    state = [(z, z, z)] * 2
+    for k, side in inward(NZ):
+        y0, y1, gp = state[side]
         here = pl.ds(k * NY, NY)
         turn = 127 - 2 * k
         al = roll(alpha, turn)
@@ -500,12 +526,15 @@
         y1 = ys_new[1] + gp * y1
         yt[here, :] = y0
         ys[here, :] = y1
-        gp = g_ref[here, :]
-
-    x0 = x1 = z
+        state[side] = y0, y1, g_ref[here, :]
+
+    middle = [pl.ds((NZ // 2 - 1 + side) * NY, NY) for side in range(2)]
+    found = [meet(*[(r_ref[middle[side], :], state[side][2], state[side][n]) for side in range(2)]) for n in range(2)]
+    state = [tuple(x[side] for x in found) for side in range(2)]
     part = max(NZ // CHUNKS, 1)
     copies = []
-    for k in reversed(range(NZ)):
+    for k, side in reversed(inward(NZ)):
+        x0, x1 = state[side]
         here = pl.ds(k * NY, NY)
         r, g = r_ref[here, :], g_ref[here, :]
         x0 = r * yt[here, :] + g * x0
@@ -513,8 +542,9 @@
         w = k < bot
         xt[here, :] = jnp.where(w, x0, 0.0)
         xs[here, :] = jnp.where(w, x1, 0.0)
-        if k % part == 0:
-            chunk = pl.ds(k * NY, part * NY)
+        state[side] = x0, x1
+        if (k + side) % part == 0:
+            chunk = pl.ds((k // part) * part * NY, part * NY)
             for n, (src, dst) in enumerate(((xt, to_ref), (xs, so_ref))):
                 copy = pltpu.make_async_copy(src.at[chunk], dst.at[chunk], sems.at[n, k // part])
                 copy.start()

time: 27.1 us -> 27 us (level)
  no operation moved by 1% of the time
where the time goes in v3:
time: 27 us; the launch traced here: 26.8 us
  starting transfers between devices  17.9 us (66%)
  Pallas kernels  7.26 us (27%)
  waiting for transfers between devices  0.97 us (4%)
  between operations  0.7 us (3%)
    ppermute x1, starting transfers between devices, per_device(): ra = lax.ppermute(msg_a, axes, first)  9.03 us
    ppermute x1, starting transfers between devices, per_device(): lax.ppermute(cols_b, 'lon', [(i, (i + 1 if i % 2 else i - 1) % count_lon)...  5.07 us
    pallas_call x1, Pallas kernels, per_device(): call(functools.partial(steps_kernel, NZ, NY, last), [SM] + [VM] * 16, [ja...  2.88 us
    pallas_call x1, Pallas kernels, per_device(): call(functools.partial(rows_kernel, NZ, NY, last), [SM] + [HB] * 7, [vmem...  2.24 us
    ppermute x1, starting transfers between devices, per_device(): ra2 = lax.ppermute(msg_a2, axes, upward)  1.92 us
    pallas_call x1, Pallas kernels, per_device(): call(functools.partial(block_kernel, NZ, NY), [VM] * 7, [flat] * 4 + [vme...  1.43 us
    ppermute x1, starting transfers between devices, per_device(): ca = lax.ppermute(cols_a, 'lon', [(i, i ^ 1) for i in range(count_lon)])  1.21 us
    ppermute x1, waiting for transfers between devices, per_device(): lax.ppermute(cols_b, 'lon', [(i, (i + 1 if i % 2 else i - 1) % count_lon)...  0.96 us
  transfers between devices with their start and end apart: 5, of which 1 were waited for; matrix products, arithmetic and copies ran while one was open for 0% of the time, Pallas kernels for 8%

profile of v3, /device:TPU:27, one launch (start us, length us, event | category | flops | bytes accessed | tf_op | source)
XLA Modules:
  0.0 26.8 jit_solution(9060322103655085420)
XLA Ops:
  0.6 2.2 %shard_map.86 = (f32[200,128]{1,0:T(8,128)S(1)}, f32[144,128]{1,0:T(8,128)S(1)}, f32[344,128]{1,0:T(8,128)S(1)}, f32[16,128]{1,0:T(8,128)S(1)}, f32[776,128]{1,0...) custom-call(s32[1]{0:T(128)} %bitcast.pos_ref, ...), custom_call_target="tpu_custom_call" | custom-call | tf_op jit(solution)/shard_map/pallas_call | solution.py:589
  2.9 0.6 %collective-permute-start.1 = (f32[344,128]{1,0:T(8,128)S(1)}, f32[344,128]{1,0:T(8,128)S(1)}, u32[]{:S(2)}, u32[]{:S(2)}) collective-permute-start(f32[344,128]{1,0:T(8,128)S(1)} %get-tuple-element.38), channel_id=1, source_target_pairs={{0,1},{1,0},{2,3},{3,2},{4,5},{5,4},{6,7},{7,6},{8,9},{9,8},{10,11... | collective-permute-start | bytes 528392 | tf_op jit(solution)/shard_map/ppermute | solution.py:597
  3.5 9.0 %collective-permute-start = (f32[200,128]{1,0:T(8,128)S(1)}, f32[200,128]{1,0:T(8,128)S(1)}, u32[]{:S(2)}, u32[]{:S(2)}) collective-permute-start(f32[200,128]{1,0:T(8,128)S(1)} %get-tuple-element.37), channel_id=1, source_target_pairs={{1,2},{2,1},{3,4},{4,3},{5,6},{6,5},{7,8},{8,7},{9,10},{10,9},{11,... | collective-permute-start | bytes 307208 | tf_op jit(solution)/shard_map/ppermute | solution.py:596
  12.6 1.9 %collective-permute-start.4 = (f32[144,128]{1,0:T(8,128)S(1)}, f32[144,128]{1,0:T(8,128)S(1)}, u32[]{:S(2)}, u32[]{:S(2)}) collective-permute-start(f32[144,128]{1,0:T(8,128)S(1)} %get-tuple-element.51), channel_id=1, source_target_pairs={{1,2},{2,1},{3,4},{4,3},{5,6},{6,5},{7,8},{8,7},{9,10},{10,9},{11,... | collective-permute-start | bytes 221192 | tf_op jit(solution)/shard_map/ppermute | solution.py:599
  14.5 1.4 %shard_map.87 = (f32[768,128]{1,0:T(8,128)S(1)}, f32[768,128]{1,0:T(8,128)S(1)}, f32[768,128]{1,0:T(8,128)S(1)}, f32[768,128]{1,0:T(8,128)S(1)}, f32[776,128]{1,...) custom-call(f32[776,128]{1,0:T(8,128)S(1)} %get-tuple-element.41.t_r, ...), custom_call_target="tpu_custom_call" | custom-call | flops 10000000 | bytes 10000000 | tf_op jit(solution)/shard_map/pallas_call | solution.py:600
  15.9 0.0 collective-permute-done.ra_ref
  15.9 0.0 collective-permute-done.1.rb_ref
  16.0 0.2 shard_map.88
  16.1 1.2 %collective-permute-start.2 = (f32[72,128]{1,0:T(8,128)S(1)}, f32[72,128]{1,0:T(8,128)S(1)}, u32[]{:S(2)}, u32[]{:S(2)}) collective-permute-start(f32[72,128]{1,0:T(8,128)S(1)} %get-tuple-element.48), channel_id=1, source_target_pairs={{0,16},{16,0},{32,48},{48,32},{64,80},{80,64},{96,112},{112,96},{1... | collective-permute-start | bytes 110600 | tf_op jit(solution)/shard_map/ppermute | solution.py:608
  17.3 5.1 %collective-permute-start.3 = (f32[72,128]{1,0:T(8,128)S(1)}, f32[72,128]{1,0:T(8,128)S(1)}, u32[]{:S(2)}, u32[]{:S(2)}) collective-permute-start(f32[72,128]{1,0:T(8,128)S(1)} %get-tuple-element.49), channel_id=1, source_target_pairs={{0,240},{16,32},{32,16},{48,64},{64,48},{80,96},{96,80},{112,128},... | collective-permute-start | bytes 110600 | tf_op jit(solution)/shard_map/ppermute | solution.py:609
  22.4 0.0 collective-permute-done.4.ra2_ref
  22.4 0.5 %shard_map.89 = (f32[768,128]{1,0:T(8,128)S(1)}, f32[768,128]{1,0:T(8,128)S(1)}, f32[768,128]{1,0:T(8,128)S(1)}, f32[768,128]{1,0:T(8,128)S(1)}, f32[768,128]{1,...) custom-call(s32[1]{0:T(128)} %bitcast.pos_ref, ...), custom_call_target="tpu_custom_call" | custom-call | flops 10000000 | bytes 10000000 | tf_op jit(solution)/shard_map/pallas_call | solution.py:611
  23.0 0.0 collective-permute-done.2.ra_ref
  23.0 1.0 %collective-permute-done.3.rb_ref = f32[72,128]{1,0:T(8,128)S(1)} collective-permute-done((f32[72,128]{1,0:T(8,128)S(1)}, f32[72,128]{1,0:T(8,128)S(1)}, u32[]{:S(2)}, u32[]{:S(2)}) %collective-permute-start.3) | collective-permute-done | bytes 36896 | tf_op jit(solution)/shard_map/ppermute | solution.py:609
  23.9 2.9 %shard_map.90 = (f32[768,128]{1,0:T(8,128)}, f32[768,128]{1,0:T(8,128)}) custom-call(s32[1]{0:T(128)} %bitcast.pos_ref, f32[72,128]{1,0:T(8,128)S(1)} %collective-permute-done.2.ra_ref, f32[72,128]{1,0:T(8,128)S(1)} %collective-permute-done.3.rb_ref, f32[96,128]{1,0:T(8,128)S(1)} %get-tuple-element.50.own_ref, f32[768,128]{1,0:T(8,128)S(1)} %get-tuple-element.58.lt_ref, ...), custom_call_target="tpu_custom_call" | custom-call | tf_op jit(solution)/shard_map/pallas_call | solution.py:616
Async XLA Ops:
  2.9 13.1 %collective-permute-start.1 = (f32[344,128]{1,0:T(8,128)S(1)}, f32[344,128]{1,0:T(8,128)S(1)}, u32[]{:S(2)}, u32[]{:S(2)}) collective-permute-start(f32[344,128]{1,0:T(8,128)S(1)} %get-tuple-element.38), channel_id=1, source_target_pairs={{0,1},{1,0},{2,3},{3,2},{4,5},{5,4},{6,7},{7,6},{8,9},{9,8},{10,11... | collective-permute-start | bytes 528392 | tf_op jit(solution)/shard_map/ppermute | solution.py:597
  3.5 12.4 %collective-permute-start = (f32[200,128]{1,0:T(8,128)S(1)}, f32[200,128]{1,0:T(8,128)S(1)}, u32[]{:S(2)}, u32[]{:S(2)}) collective-permute-start(f32[200,128]{1,0:T(8,128)S(1)} %get-tuple-element.37), channel_id=1, source_target_pairs={{1,2},{2,1},{3,4},{4,3},{5,6},{6,5},{7,8},{8,7},{9,10},{10,9},{11,... | collective-permute-start | bytes 307208 | tf_op jit(solution)/shard_map/ppermute | solution.py:596
  12.6 9.8 %collective-permute-start.4 = (f32[144,128]{1,0:T(8,128)S(1)}, f32[144,128]{1,0:T(8,128)S(1)}, u32[]{:S(2)}, u32[]{:S(2)}) collective-permute-start(f32[144,128]{1,0:T(8,128)S(1)} %get-tuple-element.51), channel_id=1, source_target_pairs={{1,2},{2,1},{3,4},{4,3},{5,6},{6,5},{7,8},{8,7},{9,10},{10,9},{11,... | collective-permute-start | bytes 221192 | tf_op jit(solution)/shard_map/ppermute | solution.py:599
  16.1 6.8 %collective-permute-start.2 = (f32[72,128]{1,0:T(8,128)S(1)}, f32[72,128]{1,0:T(8,128)S(1)}, u32[]{:S(2)}, u32[]{:S(2)}) collective-permute-start(f32[72,128]{1,0:T(8,128)S(1)} %get-tuple-element.48), channel_id=1, source_target_pairs={{0,16},{16,0},{32,48},{48,32},{64,80},{80,64},{96,112},{112,96},{1... | collective-permute-start | bytes 110600 | tf_op jit(solution)/shard_map/ppermute | solution.py:608
  17.3 6.6 %collective-permute-start.3 = (f32[72,128]{1,0:T(8,128)S(1)}, f32[72,128]{1,0:T(8,128)S(1)}, u32[]{:S(2)}, u32[]{:S(2)}) collective-permute-start(f32[72,128]{1,0:T(8,128)S(1)} %get-tuple-element.49), channel_id=1, source_target_pairs={{0,240},{16,32},{32,16},{48,64},{64,48},{80,96},{96,80},{112,128},... | collective-permute-start | bytes 110600 | tf_op jit(solution)/shard_map/ppermute | solution.py:609

commit v4 on v3

--- a/solution.py
+++ b/solution.py
@@ -77,14 +77,14 @@
 def rows_kernel(NZ, NY, last, pos_ref, *refs):
     sources, (a_ref, a2_ref, b_ref, tails_ref), kept, sems = refs[:7], refs[7:11], refs[11:18], refs[18]
     t_ref, s_ref, u_ref, v_ref, h_ref, m_ref, bot_ref = kept
-    size = NZ * NY
-    copies = []
-    for n in (6, 0, 1, 2, 4, 3, 5):
-        there = kept[n] if n == 6 else kept[n].at[pl.ds(0, size)]
-        copies.append(pltpu.make_async_copy(sources[n], there, sems.at[n]))
-        copies[-1].start()
-    for n in range(6):
-        kept[n][size:, :] = jnp.zeros((8, 128), F32)
+    copies = [pltpu.make_async_copy(sources[6], bot_ref, sems.at[6, 0])]
+    for n in (0, 1, 2, 4, 3, 5):
+        one = n in (2, 5)
+        for side, start in enumerate((0, NY - 1 if one else NY - 2)):
+            rows = pl.ds(start, 1 if one else 2)
+            copies.append(pltpu.make_async_copy(sources[n].at[:, rows, :], kept[n].at[:, rows, :], sems.at[n, side]))
+    for copy in copies:
+        copy.start()
     for copy in copies:
         copy.wait()
     j = lax.rem(pos_ref[0], last + 1)
@@ -94,7 +94,7 @@
 
     def message(row, inner, top):
         def at(ref, r):
-            return ref[pl.ds(r, NZ, stride=NY), :]
+            return ref[:, r, :]
 
         def sea(r):
             return (lev < bot_ref[r : r + 1, :]).astype(F32)
@@ -200,7 +200,8 @@
         qn_ref[pl.ds(k * NY + 8, NY), :] = qnm
         parts, wests, souths = [], [], []
         for src, c, ce in zip((t_ref, s_ref), cells, easts):
-            cn = jnp.where(sea_n, src[next_row, :], 0.0)
+            cn = src[next_row, :] if k < NZ - 1 else roll(src[here, :], -1, 0)
+            cn = jnp.where(sea_n, cn, 0.0)
             fe = pem * c + qem * ce
             fn = pnm * c + qnm * cn
             parts.append(c - fe - fn)
@@ -581,18 +582,19 @@
     last = count_lat - 1
     size = NZ * NY
     flat = vmem(size, NX)
-    fields = [a.reshape(size, NX) for a in (temp, salt, east_speed, north_speed, mixing_h, mixing_v)]
+    fields = (temp, salt, east_speed, north_speed, mixing_h, mixing_v)
     axes = ("lon", "lat")
     pos = lax.axis_index(axes).astype(jnp.int32).reshape(1)
     first, second = lat_routes(count_lon, count_lat)
 
-    msg_a, msg_a2, msg_b, tails, t, s, u, v, h, m, bot = call(
+    msg_a, msg_a2, msg_b, tails = call(
         functools.partial(rows_kernel, NZ, NY, last),
         [SM] + [HB] * 7,
-        [vmem(NFIRST * NZ + 8, NX), vmem((NF - NFIRST) * NZ, NX), vmem(NF * NZ + 8, NX), vmem(16, NX)]
-        + [vmem(size + 8, NX)] * 6 + [pltpu.VMEM((NY, NX), jnp.int32)],
-        scratch=[pltpu.SemaphoreType.DMA((7,))],
+        [vmem(NFIRST * NZ + 8, NX), vmem((NF - NFIRST) * NZ, NX), vmem(NF * NZ + 8, NX), vmem(16, NX)],
+        scratch=[vmem(NZ, NY, NX)] * 6 + [pltpu.VMEM((NY, NX), jnp.int32), pltpu.SemaphoreType.DMA((7, 2))],
     )(pos, *[pltpu.with_memory_space_constraint(a, pltpu.HBM) for a in fields], pltpu.with_memory_space_constraint(bottom, pltpu.HBM))
+    t, s, u, v, h, m = (a.reshape(size, NX) for a in fields)
+    bot = bottom
     ra = lax.ppermute(msg_a, axes, first)
     rb = lax.ppermute(msg_b, axes, second)
     upward = [(x, y) for x, y in first if NFIRST < 5 or x % count_lat % 2]

time: 27 us -> 26.8 us (level)
    pallas_call x1, Pallas kernels: 2.24 us -> 1.96 us  [per_device(): call(functools.partial(rows_kernel, NZ, NY, last), [SM] + [HB] * 7, [vmem...]
where the time goes in v4:
time: 26.8 us; the launch traced here: 26.7 us
  starting transfers between devices  17.9 us (67%)
  Pallas kernels  7.12 us (27%)
  waiting for transfers between devices  0.81 us (3%)
  between operations  0.81 us (3%)
    ppermute x1, starting transfers between devices, per_device(): ra = lax.ppermute(msg_a, axes, first)  9.03 us
    ppermute x1, starting transfers between devices, per_device(): lax.ppermute(cols_b, 'lon', [(i, (i + 1 if i % 2 else i - 1) % count_lon)...  5.07 us
    pallas_call x1, Pallas kernels, per_device(): call(functools.partial(steps_kernel, NZ, NY, last), [SM] + [VM] * 16, [ja...  2.94 us
    pallas_call x1, Pallas kernels, per_device(): call(functools.partial(rows_kernel, NZ, NY, last), [SM] + [HB] * 7, [vmem...  1.96 us
    ppermute x1, starting transfers between devices, per_device(): ra2 = lax.ppermute(msg_a2, axes, upward)  1.92 us
    pallas_call x1, Pallas kernels, per_device(): call(functools.partial(block_kernel, NZ, NY), [VM] * 7, [flat] * 4 + [vme...  1.46 us
    ppermute x1, starting transfers between devices, per_device(): ca = lax.ppermute(cols_a, 'lon', [(i, i ^ 1) for i in range(count_lon)])  1.21 us
    ppermute x1, waiting for transfers between devices, per_device(): lax.ppermute(cols_b, 'lon', [(i, (i + 1 if i % 2 else i - 1) % count_lon)...  0.8 us
  transfers between devices with their start and end apart: 5, of which 1 were waited for; matrix products, arithmetic and copies ran while one was open for 0% of the time, Pallas kernels for 8%

profile of v4, /device:TPU:27, one launch (start us, length us, event | category | flops | bytes accessed | tf_op | source)
XLA Modules:
  0.0 26.7 jit_solution(8629345880623910961)
XLA Ops:
  0.6 0.0 copy-start
  0.6 0.0 copy-start.1
  0.7 0.0 copy-start.2
  0.7 0.0 copy-start.3
  0.7 0.0 copy-start.4
  0.7 0.0 copy-start.5
  0.7 2.0 %shard_map.86 = (f32[200,128]{1,0:T(8,128)S(1)}, f32[144,128]{1,0:T(8,128)S(1)}, f32[344,128]{1,0:T(8,128)S(1)}, f32[16,128]{1,0:T(8,128)S(1)}) custom-call(s32[1]{0:T(128)} %bitcast.pos_ref, f32[48,16,128]{2,1,0:T(8,128)} %refs_0_.1, f32[48,16,128]{2,1,0:T(8,128)} %refs_1_.1, f32[48,16,128]{2,1,0:T(8,128)} %refs_2_.1, f32[48,16,128]{2,1,0:T(8,128)} %refs_3_.1, ...), custom_call_target="tpu_custom_call" | custom-call | tf_op jit(solution)/shard_map/pallas_call | solution.py:590
  2.7 0.0 copy-start.6
  2.7 0.6 %collective-permute-start.1 = (f32[344,128]{1,0:T(8,128)S(1)}, f32[344,128]{1,0:T(8,128)S(1)}, u32[]{:S(2)}, u32[]{:S(2)}) collective-permute-start(f32[344,128]{1,0:T(8,128)S(1)} %get-tuple-element.31), channel_id=1, source_target_pairs={{0,1},{1,0},{2,3},{3,2},{4,5},{5,4},{6,7},{7,6},{8,9},{9,8},{10,11... | collective-permute-start | bytes 528392 | tf_op jit(solution)/shard_map/ppermute | solution.py:599
  3.3 9.0 %collective-permute-start = (f32[200,128]{1,0:T(8,128)S(1)}, f32[200,128]{1,0:T(8,128)S(1)}, u32[]{:S(2)}, u32[]{:S(2)}) collective-permute-start(f32[200,128]{1,0:T(8,128)S(1)} %get-tuple-element.30), channel_id=1, source_target_pairs={{1,2},{2,1},{3,4},{4,3},{5,6},{6,5},{7,8},{8,7},{9,10},{10,9},{11,... | collective-permute-start | bytes 307208 | tf_op jit(solution)/shard_map/ppermute | solution.py:598
  12.4 1.9 %collective-permute-start.4 = (f32[144,128]{1,0:T(8,128)S(1)}, f32[144,128]{1,0:T(8,128)S(1)}, u32[]{:S(2)}, u32[]{:S(2)}) collective-permute-start(f32[144,128]{1,0:T(8,128)S(1)} %get-tuple-element.37), channel_id=1, source_target_pairs={{1,2},{2,1},{3,4},{4,3},{5,6},{6,5},{7,8},{8,7},{9,10},{10,9},{11,... | collective-permute-start | bytes 221192 | tf_op jit(solution)/shard_map/ppermute | solution.py:601
  14.3 0.0 copy-done
  14.3 0.0 copy-done.1
  14.3 0.0 copy-done.2
  14.3 0.0 copy-done.3
  14.3 0.0 copy-done.4
  14.3 0.0 copy-done.5
  14.4 0.0 copy-done.6
  14.4 1.5 %shard_map.87 = (f32[768,128]{1,0:T(8,128)S(1)}, f32[768,128]{1,0:T(8,128)S(1)}, f32[768,128]{1,0:T(8,128)S(1)}, f32[768,128]{1,0:T(8,128)S(1)}, f32[776,128]{1,...) custom-call(f32[768,128]{1,0:T(8,128)S(1)} %bitcast.9, ...), custom_call_target="tpu_custom_call" | custom-call | flops 10000000 | bytes 10000000 | tf_op jit(solution)/shard_map/pallas_call | solution.py:602
  15.8 0.0 collective-permute-done.ra_ref
  15.8 0.0 collective-permute-done.1.rb_ref
  15.9 0.2 shard_map.88
  16.0 1.2 %collective-permute-start.2 = (f32[72,128]{1,0:T(8,128)S(1)}, f32[72,128]{1,0:T(8,128)S(1)}, u32[]{:S(2)}, u32[]{:S(2)}) collective-permute-start(f32[72,128]{1,0:T(8,128)S(1)} %get-tuple-element.34), channel_id=1, source_target_pairs={{0,16},{16,0},{32,48},{48,32},{64,80},{80,64},{96,112},{112,96},{1... | collective-permute-start | bytes 110600 | tf_op jit(solution)/shard_map/ppermute | solution.py:610
  17.2 5.1 %collective-permute-start.3 = (f32[72,128]{1,0:T(8,128)S(1)}, f32[72,128]{1,0:T(8,128)S(1)}, u32[]{:S(2)}, u32[]{:S(2)}) collective-permute-start(f32[72,128]{1,0:T(8,128)S(1)} %get-tuple-element.35), channel_id=1, source_target_pairs={{0,240},{16,32},{32,16},{48,64},{64,48},{80,96},{96,80},{112,128},... | collective-permute-start | bytes 110600 | tf_op jit(solution)/shard_map/ppermute | solution.py:611
  22.3 0.0 collective-permute-done.4.ra2_ref
  22.3 0.6 %shard_map.89 = (f32[768,128]{1,0:T(8,128)S(1)}, f32[768,128]{1,0:T(8,128)S(1)}, f32[768,128]{1,0:T(8,128)S(1)}, f32[768,128]{1,0:T(8,128)S(1)}, f32[768,128]{1,...) custom-call(s32[1]{0:T(128)} %bitcast.pos_ref, ...), custom_call_target="tpu_custom_call" | custom-call | flops 10000000 | bytes 10000000 | tf_op jit(solution)/shard_map/pallas_call | solution.py:613
  22.9 0.0 collective-permute-done.2.ra_ref
  22.9 0.8 %collective-permute-done.3.rb_ref = f32[72,128]{1,0:T(8,128)S(1)} collective-permute-done((f32[72,128]{1,0:T(8,128)S(1)}, f32[72,128]{1,0:T(8,128)S(1)}, u32[]{:S(2)}, u32[]{:S(2)}) %collective-permute-start.3) | collective-permute-done | bytes 36896 | tf_op jit(solution)/shard_map/ppermute | solution.py:611
  23.7 2.9 %shard_map.90 = (f32[768,128]{1,0:T(8,128)}, f32[768,128]{1,0:T(8,128)}) custom-call(s32[1]{0:T(128)} %bitcast.pos_ref, f32[72,128]{1,0:T(8,128)S(1)} %collective-permute-done.2.ra_ref, f32[72,128]{1,0:T(8,128)S(1)} %collective-permute-done.3.rb_ref, f32[96,128]{1,0:T(8,128)S(1)} %get-tuple-element.36.own_ref, f32[768,128]{1,0:T(8,128)S(1)} %get-tuple-element.44.lt_ref, ...), custom_call_target="tpu_custom_call" | custom-call | tf_op jit(solution)/shard_map/pallas_call | solution.py:618
Async XLA Ops:
  0.6 13.7 %copy-start = (f32[48,16,128]{2,1,0:T(8,128)S(1)}, f32[48,16,128]{2,1,0:T(8,128)}, u32[]{:S(2)}) copy-start(f32[48,16,128]{2,1,0:T(8,128)} %refs_0_.1) | copy-start | bytes 1179652
  0.6 13.7 %copy-start.1 = (f32[48,16,128]{2,1,0:T(8,128)S(1)}, f32[48,16,128]{2,1,0:T(8,128)}, u32[]{:S(2)}) copy-start(f32[48,16,128]{2,1,0:T(8,128)} %refs_1_.1) | copy-start | bytes 1179652
  0.7 13.7 %copy-start.2 = (f32[48,16,128]{2,1,0:T(8,128)S(1)}, f32[48,16,128]{2,1,0:T(8,128)}, u32[]{:S(2)}) copy-start(f32[48,16,128]{2,1,0:T(8,128)} %refs_3_.1) | copy-start | bytes 1179652
  0.7 13.7 %copy-start.3 = (f32[48,16,128]{2,1,0:T(8,128)S(1)}, f32[48,16,128]{2,1,0:T(8,128)}, u32[]{:S(2)}) copy-start(f32[48,16,128]{2,1,0:T(8,128)} %refs_4_.1) | copy-start | bytes 1179652
  0.7 13.7 %copy-start.4 = (f32[48,16,128]{2,1,0:T(8,128)S(1)}, f32[48,16,128]{2,1,0:T(8,128)}, u32[]{:S(2)}) copy-start(f32[48,16,128]{2,1,0:T(8,128)} %refs_2_.1) | copy-start | bytes 1179652
  0.7 13.7 %copy-start.5 = (f32[48,16,128]{2,1,0:T(8,128)S(1)}, f32[48,16,128]{2,1,0:T(8,128)}, u32[]{:S(2)}) copy-start(f32[48,16,128]{2,1,0:T(8,128)} %refs_5_.1) | copy-start | bytes 1179652
  2.7 11.7 %copy-start.6 = (s32[16,128]{1,0:T(8,128)S(1)}, s32[16,128]{1,0:T(8,128)}, u32[]{:S(2)}) copy-start(s32[16,128]{1,0:T(8,128)} %bot_ref.7) | copy-start | bytes 24580
  2.7 13.2 %collective-permute-start.1 = (f32[344,128]{1,0:T(8,128)S(1)}, f32[344,128]{1,0:T(8,128)S(1)}, u32[]{:S(2)}, u32[]{:S(2)}) collective-permute-start(f32[344,128]{1,0:T(8,128)S(1)} %get-tuple-element.31), channel_id=1, source_target_pairs={{0,1},{1,0},{2,3},{3,2},{4,5},{5,4},{6,7},{7,6},{8,9},{9,8},{10,11... | collective-permute-start | bytes 528392 | tf_op jit(solution)/shard_map/ppermute | solution.py:599
  3.3 12.5 %collective-permute-start = (f32[200,128]{1,0:T(8,128)S(1)}, f32[200,128]{1,0:T(8,128)S(1)}, u32[]{:S(2)}, u32[]{:S(2)}) collective-permute-start(f32[200,128]{1,0:T(8,128)S(1)} %get-tuple-element.30), channel_id=1, source_target_pairs={{1,2},{2,1},{3,4},{4,3},{5,6},{6,5},{7,8},{8,7},{9,10},{10,9},{11,... | collective-permute-start | bytes 307208 | tf_op jit(solution)/shard_map/ppermute | solution.py:598
  12.4 9.9 %collective-permute-start.4 = (f32[144,128]{1,0:T(8,128)S(1)}, f32[144,128]{1,0:T(8,128)S(1)}, u32[]{:S(2)}, u32[]{:S(2)}) collective-permute-start(f32[144,128]{1,0:T(8,128)S(1)} %get-tuple-element.37), channel_id=1, source_target_pairs={{1,2},{2,1},{3,4},{4,3},{5,6},{6,5},{7,8},{8,7},{9,10},{10,9},{11,... | collective-permute-start | bytes 221192 | tf_op jit(solution)/shard_map/ppermute | solution.py:601
  16.0 6.9 %collective-permute-start.2 = (f32[72,128]{1,0:T(8,128)S(1)}, f32[72,128]{1,0:T(8,128)S(1)}, u32[]{:S(2)}, u32[]{:S(2)}) collective-permute-start(f32[72,128]{1,0:T(8,128)S(1)} %get-tuple-element.34), channel_id=1, source_target_pairs={{0,16},{16,0},{32,48},{48,32},{64,80},{80,64},{96,112},{112,96},{1... | collective-permute-start | bytes 110600 | tf_op jit(solution)/shard_map/ppermute | solution.py:610
  17.2 6.5 %collective-permute-start.3 = (f32[72,128]{1,0:T(8,128)S(1)}, f32[72,128]{1,0:T(8,128)S(1)}, u32[]{:S(2)}, u32[]{:S(2)}) collective-permute-start(f32[72,128]{1,0:T(8,128)S(1)} %get-tuple-element.35), channel_id=1, source_target_pairs={{0,240},{16,32},{32,16},{48,64},{64,48},{80,96},{96,80},{112,128},... | collective-permute-start | bytes 110600 | tf_op jit(solution)/shard_map/ppermute | solution.py:611
